TPU v7x, 32 devices: a whole 2x2x4 slice. The times are simulated.
32 devices in a mesh: section: 2 (over core), dp: 4 (over y, x), shard: 4 (over z).
Axes of the slice: x: 2, y: 2, z: 4, core: 2. Of those that a mesh axis runs over, the one named last changes fastest.
Arguments:
- boundary: bfloat16 [2, 4, 4, 1024, 1024], P('section', None, 'shard', 'dp'), may hold values from -6 to 6
- first_len: int32 [4, 4], P(None, 'shard'), may hold values from 256 to 1024, as said below
- qkv_weight: bfloat16 [2, 1024, 3072], P('section', 'shard'), may hold values from -0.1875 to 0.1875
- out_weight: bfloat16 [2, 1024, 1024], P('section', 'shard'), may hold values from -0.1875 to 0.1875
- up_weight: bfloat16 [2, 1024, 4096], P('section', 'shard'), may hold values from -0.1875 to 0.1875
- down_weight: bfloat16 [2, 4096, 1024], P('section', 'shard'), may hold values from -0.09375 to 0.09375
- norm_gain: float32 [2, 3, 1024], P('section'), may hold values from 0.5 to 1.5
- norm_shift: float32 [2, 3, 1024], P('section'), may hold values from -1.5 to 1.5
- mid_gain: float32 [2, 4096], P('section'), may hold values from 0.5 to 1.5
- mid_shift: float32 [2, 4096], P('section'), may hold values from -1.5 to 1.5
- head_scale: float32 [2, 16], P('section'), may hold values from 0.25 to 1.75
Outputs:
- ends: bfloat16 [2, 4, 4, 1024, 1024], P('section', None, 'shard', 'dp')
- grad_qkv: float32 [2, 1024, 3072], P('section', 'shard')
- grad_out: float32 [2, 1024, 1024], P('section', 'shard')
- grad_up: float32 [2, 1024, 4096], P('section', 'shard')
- grad_down: float32 [2, 4096, 1024], P('section', 'shard')
- grad_norm_gain: float32 [2, 3, 1024], P('section')
- grad_norm_shift: float32 [2, 3, 1024], P('section')
- grad_mid_gain: float32 [2, 4096], P('section')
- grad_mid_shift: float32 [2, 4096], P('section')
- grad_head_scale: float32 [2, 16], P('section')
Inputs may be any that keep to these rules, and one draw needn't show every extreme that they name: The first document runs from position 0 to first_len - 1 and the second fills the rest of the stream (empty when first_len = 1024). For every stream index g, at least one micro-batch has first_len = 1024.
All inputs are finite; a program needn't handle non-finite values.
Results may differ from a plain program's by a relative error of at most 0.015.
Values may be sent and summed in bfloat16 or wider, within the bound.
A program may use at most 320 MiB of HBM per device.

v0:
```python
import math

import jax
import jax.numpy as jnp
from jax import lax
from jax.sharding import PartitionSpec as P

EPSILON = 1e-05


def shifted(value, axis, steps):
    count = lax.axis_size(axis)
    first, last = (max(0, -steps), min(count, count - steps))
    return lax.ppermute(value, axis, [(source, source + steps) for source in range(first, last)])


def normalize(values_in, gain, shift):
    centre = values_in - jnp.mean(values_in, axis=-1, keepdims=True)
    spread = jnp.mean(centre * centre, axis=-1, keepdims=True)
    return centre * lax.rsqrt(spread + EPSILON) * gain + shift


def middle_norm(hidden, mid_gain, mid_shift):
    return normalize(jax.nn.gelu(hidden, approximate=False), mid_gain, mid_shift)


def contract_rows(left, right):
    return lax.dot_general(
        left, right, (((0,), (0,)), ((), ())), preferred_element_type=jnp.float32
    )


def contract_cols(left, right):
    return lax.dot_general(
        left, right, (((1,), (1,)), ((), ())), preferred_element_type=jnp.float32
    )


def visible(query_place, key_place, split_at):
    same_doc = (query_place[:, None] < split_at) == (key_place[None, :] < split_at)
    return same_doc & (key_place[None, :] <= query_place[:, None])


def forward_parts(stream_in, weights, small, split_at, head_count):
    weight_qkv, weight_out, weight_up, weight_down = weights
    gains, shifts, mid_gain, mid_shift, head_scale = small
    row_count, model_width = stream_in.shape
    head_dim = model_width // head_count
    factor = 1.0 / math.sqrt(head_dim)
    normed = normalize(stream_in, gains[0], shifts[0]).astype(jnp.bfloat16)
    projected = jnp.dot(normed, weight_qkv, preferred_element_type=jnp.float32).astype(jnp.bfloat16)
    queries = projected[:, :model_width].reshape(row_count, head_count, head_dim)
    key_rows = projected[:, model_width : 2 * model_width].reshape(row_count, head_count, head_dim)
    value_rows = projected[:, 2 * model_width :].reshape(row_count, head_count, head_dim)
    keys_all, values_all = (
        lax.all_gather(key_rows, "dp", axis=0, tiled=True),
        lax.all_gather(value_rows, "dp", axis=0, tiled=True),
    )
    seq_len = keys_all.shape[0]
    own_place = lax.axis_index("dp") * row_count + jnp.arange(row_count, dtype=jnp.int32)
    all_place = jnp.arange(seq_len, dtype=jnp.int32)
    allowed = visible(own_place, all_place, split_at)
    scores = (
        jnp.einsum("qhd,khd->hqk", queries, keys_all, preferred_element_type=jnp.float32) * factor
    )
    scores = jnp.where(allowed[None], scores, -1e30)
    row_max = jnp.max(scores, axis=-1, keepdims=True)
    log_total = row_max + jnp.log(jnp.sum(jnp.exp(scores - row_max), axis=-1, keepdims=True))
    attend = jnp.exp(scores - log_total)
    attend_low = attend.astype(jnp.bfloat16)
    head_out = jnp.einsum(
        "hqk,khd->qhd", attend_low, values_all, preferred_element_type=jnp.float32
    )
    scaled = (
        (head_out * head_scale[None, :, None]).astype(jnp.bfloat16).reshape(row_count, model_width)
    )
    branch = jnp.dot(scaled, weight_out, preferred_element_type=jnp.float32)
    residual = stream_in + normalize(branch, gains[1], shifts[1])
    ffn_input = normalize(residual, gains[2], shifts[2]).astype(jnp.bfloat16)
    hidden = jnp.dot(ffn_input, weight_up, preferred_element_type=jnp.float32)
    middle = middle_norm(hidden, mid_gain, mid_shift).astype(jnp.bfloat16)
    return dict(
        normed=normed,
        queries=queries,
        key_rows=key_rows,
        value_rows=value_rows,
        keys_all=keys_all,
        values_all=values_all,
        own_place=own_place,
        all_place=all_place,
        attend=attend,
        attend_low=attend_low,
        log_total=log_total,
        head_out=head_out,
        scaled=scaled,
        branch=branch,
        residual=residual,
        ffn_input=ffn_input,
        hidden=hidden,
        middle=middle,
        factor=factor,
    )


def backward_parts(stream_in, grad_in, weights, small, split_at, head_count):
    weight_qkv, weight_out, weight_up, weight_down = weights
    gains, shifts, mid_gain, mid_shift, head_scale = small
    parts = forward_parts(stream_in, weights, small, split_at, head_count)
    row_count, model_width = stream_in.shape
    head_dim = model_width // head_count
    factor = parts["factor"]
    grad_down = contract_rows(parts["middle"], grad_in)
    d_middle = contract_cols(grad_in, weight_down)
    unused, pull_middle = jax.vjp(middle_norm, parts["hidden"], mid_gain, mid_shift)
    d_hidden, grad_mid_gain, grad_mid_shift = pull_middle(d_middle)
    d_hidden = d_hidden.astype(jnp.bfloat16)
    grad_up = contract_rows(parts["ffn_input"], d_hidden)
    d_ffn_input = contract_cols(d_hidden, weight_up)
    unused, pull_third = jax.vjp(normalize, parts["residual"], gains[2], shifts[2])
    d_residual, gain_third, shift_third = pull_third(d_ffn_input)
    d_residual = d_residual + grad_in.astype(jnp.float32)
    unused, pull_second = jax.vjp(normalize, parts["branch"], gains[1], shifts[1])
    d_branch, gain_second, shift_second = pull_second(d_residual)
    d_branch = d_branch.astype(jnp.bfloat16)
    grad_out = contract_rows(parts["scaled"], d_branch)
    d_scaled = contract_cols(d_branch, weight_out).reshape(row_count, head_count, head_dim)
    grad_head_scale = jnp.sum(d_scaled * parts["head_out"], axis=(0, 2))
    d_heads = (d_scaled * head_scale[None, :, None]).astype(jnp.bfloat16)
    attend = parts["attend"]
    d_attend = jnp.einsum(
        "qhd,khd->hqk", d_heads, parts["values_all"], preferred_element_type=jnp.float32
    )
    row_dot = jnp.sum(attend * d_attend, axis=-1, keepdims=True)
    d_scores = (attend * (d_attend - row_dot)).astype(jnp.bfloat16)
    d_query = (
        jnp.einsum("hqk,khd->qhd", d_scores, parts["keys_all"], preferred_element_type=jnp.float32)
        * factor
    ).astype(jnp.bfloat16)
    full_keys = (
        jnp.einsum("hqk,qhd->khd", d_scores, parts["queries"], preferred_element_type=jnp.float32)
        * factor
    )
    full_values = jnp.einsum(
        "hqk,qhd->khd", parts["attend_low"], d_heads, preferred_element_type=jnp.float32
    )
    d_keys, d_values = (
        lax.psum_scatter(full_keys, "dp", scatter_dimension=0, tiled=True),
        lax.psum_scatter(full_values, "dp", scatter_dimension=0, tiled=True),
    )
    d_projected = jnp.concatenate(
        [
            d_query.reshape(row_count, model_width),
            d_keys.astype(jnp.bfloat16).reshape(row_count, model_width),
            d_values.astype(jnp.bfloat16).reshape(row_count, model_width),
        ],
        axis=1,
    )
    grad_qkv = contract_rows(parts["normed"], d_projected)
    d_normed = contract_cols(d_projected, weight_qkv)
    unused, pull_first = jax.vjp(normalize, stream_in, gains[0], shifts[0])
    d_entry, gain_first, shift_first = pull_first(d_normed)
    d_entry = d_entry + d_residual
    big_grads = (grad_qkv, grad_out, grad_up, grad_down)
    small_grads = (
        jnp.stack([gain_first, gain_second, gain_third]),
        jnp.stack([shift_first, shift_second, shift_third]),
        grad_mid_gain,
        grad_mid_shift,
        grad_head_scale,
    )
    return (d_entry, big_grads, small_grads)


def add_up(first_term, second_term):
    return first_term + second_term


def local(
    boundary,
    first_len,
    qkv_weight,
    out_weight,
    up_weight,
    down_weight,
    norm_gain,
    norm_shift,
    mid_gain,
    mid_shift,
    head_scale,
):
    section_index = lax.axis_index("section")
    gathered = (
        lax.all_gather(qkv_weight, "shard", axis=1, tiled=True),
        lax.all_gather(out_weight, "shard", axis=1, tiled=True),
        lax.all_gather(up_weight, "shard", axis=1, tiled=True),
        lax.all_gather(down_weight, "shard", axis=1, tiled=True),
    )
    weights = tuple((piece[0] for piece in gathered))
    small = (norm_gain[0], norm_shift[0], mid_gain[0], mid_shift[0], head_scale[0])
    head_count = head_scale.shape[1]
    micro = boundary.shape[1]
    row_count = boundary.shape[3]
    model_width = boundary.shape[4]
    local_ends = boundary[0, :, 0]
    splits = first_len[:, 0]

    def forward_tick(step_index, carry):
        incoming, kept, ends = carry
        index = step_index - section_index
        active = (index >= 0) & (index < micro)
        slot = jnp.clip(index, 0, micro - 1)
        entry = jnp.where(section_index == 0, local_ends[slot], incoming)
        parts = forward_parts(entry.astype(jnp.float32), weights, small, splits[slot], head_count)
        result = (
            parts["residual"]
            + jnp.dot(parts["middle"], weights[3], preferred_element_type=jnp.float32)
        ).astype(jnp.bfloat16)
        kept = kept.at[slot].set(jnp.where(active, entry, kept[slot]))
        ends = ends.at[slot].set(jnp.where(active, result, ends[slot]))
        incoming = shifted(result, "section", 1)
        return (incoming, kept, ends)

    blank = jnp.zeros((row_count, model_width), jnp.bfloat16)
    stack_blank = jnp.zeros((micro, row_count, model_width), jnp.bfloat16)
    unused, kept, ends = lax.fori_loop(
        0, micro + 1, forward_tick, (blank, stack_blank, stack_blank)
    )

    def backward_tick(step_index, carry):
        incoming, ends, big_sums, small_sums = carry
        index = micro - step_index - section_index
        active = (index >= 0) & (index < micro)
        slot = jnp.clip(index, 0, micro - 1)
        grad_in = jnp.where(section_index == 1, local_ends[slot], incoming)
        grad_in = jnp.where(active, grad_in, jnp.zeros_like(grad_in))
        d_entry, big_grads, small_grads = backward_parts(
            kept[slot].astype(jnp.float32), grad_in, weights, small, splits[slot], head_count
        )
        d_low = d_entry.astype(jnp.bfloat16)
        ends = ends.at[slot].set(jnp.where(active & (section_index == 0), d_low, ends[slot]))
        big_sums = jax.tree.map(add_up, big_sums, big_grads)
        small_sums = jax.tree.map(add_up, small_sums, small_grads)
        incoming = shifted(d_low, "section", -1)
        return (incoming, ends, big_sums, small_sums)

    big_zero = tuple((jnp.zeros(item.shape, jnp.float32) for item in weights))
    small_zero = tuple((jnp.zeros(item.shape, jnp.float32) for item in small))
    unused, ends, big_sums, small_sums = lax.fori_loop(
        0, micro + 1, backward_tick, (blank, ends, big_zero, small_zero)
    )
    shares = (
        lax.psum_scatter(big_sums[0][None], "shard", scatter_dimension=1, tiled=True),
        lax.psum_scatter(big_sums[1][None], "shard", scatter_dimension=1, tiled=True),
        lax.psum_scatter(big_sums[2][None], "shard", scatter_dimension=1, tiled=True),
        lax.psum_scatter(big_sums[3][None], "shard", scatter_dimension=1, tiled=True),
    )
    shares = lax.psum((shares[0], shares[1], shares[2], shares[3]), "dp")
    totals = lax.psum(
        (small_sums[0], small_sums[1], small_sums[2], small_sums[3], small_sums[4]), ("dp", "shard")
    )
    return (
        ends[None, :, None],
        shares[0],
        shares[1],
        shares[2],
        shares[3],
        totals[0][None],
        totals[1][None],
        totals[2][None],
        totals[3][None],
        totals[4][None],
    )


def solution(mesh):
    placed = (
        P("section", None, "shard", "dp", None),
        P(None, "shard"),
        P("section", "shard", None),
        P("section", "shard", None),
        P("section", "shard", None),
        P("section", "shard", None),
        P("section", None, None),
        P("section", None, None),
        P("section", None),
        P("section", None),
        P("section", None),
    )
    return jax.shard_map(
        local,
        mesh=mesh,
        in_specs=placed,
        out_specs=(
            P("section", None, "shard", "dp", None),
            P("section", "shard", None),
            P("section", "shard", None),
            P("section", "shard", None),
            P("section", "shard", None),
            P("section", None, None),
            P("section", None, None),
            P("section", None),
            P("section", None),
            P("section", None),
        ),
        check_vma=False,
    )
```

profile of v0, /device:TPU:8, one launch (start us, length us, event | category | flops | bytes accessed | tf_op | source)
XLA Modules:
  0.0 3571.0 jit_solution(794900597879809280)
XLA Ops:
  10.2 45.0 %all-gather.11.cloned.1.call-done = bf16[1,1024,1024]{2,1,0:T(8,128)(2,1)} async-done(((bf16[1,256,1024]{2,1,0:T(8,128)(2,1)}), bf16[1,1024,1024]{2,1,0:T(8,128)(2,1)}) %all-gather.11.cloned.1.call-update) | async-done | bytes 2097168 | tf_op jit(solution)/shard_map/all_gather | solution.py:194
  55.1 114.3 %all-gather.9.cloned.1.call-done = bf16[1,1024,3072]{2,1,0:T(8,128)(2,1)} async-done(((bf16[1,256,3072]{2,1,0:T(8,128)(2,1)}), bf16[1,1024,3072]{2,1,0:T(8,128)(2,1)}) %all-gather.9.cloned.1.call-update) | async-done | bytes 6291472 | tf_op jit(solution)/shard_map/all_gather | solution.py:193
  169.4 149.5 %all-gather.13.cloned.1.call-done = bf16[1,1024,4096]{2,1,0:T(8,128)(2,1)} async-done(((bf16[1,256,4096]{2,1,0:T(8,128)(2,1)}), bf16[1,1024,4096]{2,1,0:T(8,128)(2,1)}) %all-gather.13.cloned.1.call-update) | async-done | bytes 8388624 | tf_op jit(solution)/shard_map/all_gather | solution.py:195
  318.9 149.3 %all-gather.15.cloned.1.call-done = bf16[1,4096,1024]{2,1,0:T(8,128)(2,1)} async-done(((bf16[1,1024,1024]{2,1,0:T(8,128)(2,1)}), bf16[1,4096,1024]{2,1,0:T(8,128)(2,1)}) %all-gather.15.cloned.1.call-update) | async-done | bytes 8388624 | tf_op jit(solution)/shard_map/all_gather | solution.py:196
  472.3 594.4 %while.56 = (s32[]{:T(128)}, bf16[256,1024]{1,0:T(8,128)(2,1)}, bf16[4,256,1024]{2,1,0:T(8,128)(2,1)}, bf16[4,256,1024]{2,1,0:T(8,128)(2,1)}, pred[]{:T(512)}, /...) while((s32[]{:T(128)}, bf16[256,1024]{1,0:T(8,128)(2,1)}, ...), condition=%wide.region_12.13_spmd, body=%wide.region_0.12_spmd.sunk | while | flops 7650933248 | bytes 258215680 | solution.py:225
  491.5 31.2 all-gather.19.cloned.1.call-done
  533.5 26.8 all-gather.17.cloned.1.call-done
  570.9 11.4 fusion.221
  611.1 30.2 all-gather.19.cloned.1.call-done
  652.1 26.9 all-gather.17.cloned.1.call-done
  689.7 11.4 fusion.221
  729.9 30.2 all-gather.19.cloned.1.call-done
  770.9 26.8 all-gather.17.cloned.1.call-done
  808.3 11.4 fusion.221
  848.5 30.2 all-gather.19.cloned.1.call-done
  889.6 26.8 all-gather.17.cloned.1.call-done
  926.9 11.4 fusion.221
  967.1 30.2 all-gather.19.cloned.1.call-done
  1008.2 26.8 all-gather.17.cloned.1.call-done
  1045.5 11.4 fusion.221
  1067.5 1374.7 %while.57 = (s32[]{:T(128)}, bf16[256,1024]{1,0:T(8,128)(2,1)}, bf16[4,256,1024]{2,1,0:T(8,128)(2,1)}, f32[1024,3072]{1,0:T(8,128)}, f32[1024,1024]{1,0:T(8,128)...) while((s32[]{:T(128)}, bf16[256,1024]{1,0:T(8,128)(2,1)}, ...), condition=%wide.region_45.46_spmd.clone, body=%wide.region_13.45_spmd.clone.sunk | while | flops 20692625408 | bytes 826313728 | solution.py:248
  1085.0 29.5 all-gather.23.cloned.1.call-done
  1125.1 27.0 all-gather.21.cloned.1.call-done
  1164.5 16.0 fusion.259
  1211.3 14.4 multiply_reduce_fusion.34
  1225.8 12.9 multiply_convert_fusion.10
  1278.1 41.5 %reduce-scatter.17.cloned.1.call-done = f32[256,16,64]{0,2,1:T(8,128)} async-done(((f32[1024,16,64]{0,2,1:T(8,128)}), f32[256,16,64]{0,2,1:T(8,128)}) %reduce-scatter.17.cloned.1.call-update) | async-done | bytes 1048592 | tf_op jit(solution)/shard_map/while/body/eval_jaxpr/reduce_scatter | solution.py:147
  1356.6 30.3 all-gather.23.cloned.1.call-done
  1397.5 26.9 all-gather.21.cloned.1.call-done
  1436.9 16.2 fusion.259
  1483.7 14.4 multiply_reduce_fusion.34
  1498.1 12.9 multiply_convert_fusion.10
  1533.4 14.8 select_add_fusion.13
  1548.3 11.3 select_add_fusion.14
  1560.9 31.2 reduce-scatter.17.cloned.1.call-done
  1631.9 30.2 all-gather.23.cloned.1.call-done
  1673.1 26.7 all-gather.21.cloned.1.call-done
  1712.2 15.9 fusion.259
  1758.8 14.4 multiply_reduce_fusion.34
  1773.2 12.9 multiply_convert_fusion.10
  1808.5 14.8 select_add_fusion.13
  1823.4 11.3 select_add_fusion.14
  1836.0 31.1 reduce-scatter.17.cloned.1.call-done
  1907.0 30.2 all-gather.23.cloned.1.call-done
  1947.8 27.2 all-gather.21.cloned.1.call-done
  1987.4 16.0 fusion.259
  2034.2 14.4 multiply_reduce_fusion.34
  2048.6 12.9 multiply_convert_fusion.10
  2084.0 14.8 select_add_fusion.13
  2111.4 31.1 reduce-scatter.17.cloned.1.call-done
  2182.2 30.2 all-gather.23.cloned.1.call-done
  2223.1 27.1 all-gather.21.cloned.1.call-done
  2262.6 16.2 fusion.259
  2309.5 14.4 multiply_reduce_fusion.34
  2323.9 12.9 multiply_convert_fusion.10
  2359.2 14.8 select_add_fusion.13
  2374.1 11.3 select_add_fusion.14
  2386.7 31.2 reduce-scatter.17.cloned.1.call-done
  2444.9 78.6 %reduce-scatter.9.cloned.1.call-done = f32[1,256,1024]{2,1,0:T(8,128)} async-done(((f32[1,1024,1024]{2,1,0:T(8,128)}), f32[1,256,1024]{2,1,0:T(8,128)}) %reduce-scatter.9.cloned.1.call-update) | async-done | bytes 1048592 | tf_op jit(solution)/shard_map/reduce_scatter | solution.py:253
  2523.5 214.7 %reduce-scatter.7.cloned.1.call-done = f32[1,256,3072]{2,1,0:T(8,128)} async-done(((f32[1,1024,3072]{2,1,0:T(8,128)}), f32[1,256,3072]{2,1,0:T(8,128)}) %reduce-scatter.7.cloned.1.call-update) | async-done | bytes 3145744 | tf_op jit(solution)/shard_map/reduce_scatter | solution.py:252
  2738.2 280.5 %reduce-scatter.11.cloned.1.call-done = f32[1,256,4096]{2,1,0:T(8,128)} async-done(((f32[1,1024,4096]{2,1,0:T(8,128)}), f32[1,256,4096]{2,1,0:T(8,128)}) %reduce-scatter.11.cloned.1.call-update) | async-done | bytes 4194320 | tf_op jit(solution)/shard_map/reduce_scatter | solution.py:254
  3018.7 283.4 %reduce-scatter.13.cloned.1.call-done = f32[1,1024,1024]{2,1,0:T(8,128)} async-done(((f32[1,4096,1024]{2,1,0:T(8,128)}), f32[1,1024,1024]{2,1,0:T(8,128)}) %reduce-scatter.13.cloned.1.call-update) | async-done | bytes 4194320 | tf_op jit(solution)/shard_map/reduce_scatter | solution.py:255
  3302.9 76.8 %all-reduce = (f32[1,3,1024]{2,0,1:T(1,128)}, f32[1,3,1024]{2,0,1:T(1,128)}, f32[1,4096]{1,0:T(1,128)}, f32[1,4096]{1,0:T(1,128)}, f32[1,16]{1,0:T(1,128)}) all-reduce(f32[1,3,1024]{2,0,1:T(1,128)S(1)} %broadcast_in_dim.273, f32[1,3,1024]{2,0,1:T(1,128)S(1)} %broadcast_in_dim.274, ...), channel_id=1, replica_groups=mesh['section'=2,'dp'=4,'shard'=4] {'dp','shard'}, use_global_device_ids=true, to_apply=%region_54.55 | all-reduce | flops 14352 | bytes 114816 | tf_op jit(solution)/shard_map/psum | solution.py:258
  3379.7 173.4 %all-reduce.4.cloned.1.call-done = (f32[1,256,3072]{2,1,0:T(8,128)}, f32[1,256,1024]{2,1,0:T(8,128)}, f32[1,256,4096]{2,1,0:T(8,128)}, f32[1,1024,1024]{2,1,0:T(8,128)}) async-done(((f32[1,256,3072]{2,1,0:T(8,128)}, f32[1,256,1024]{2,1,0:T(8,128)}, f32[1,256,4096]{2,1,0:T(8,128)}, f32[1,1024,1024]{2,1,0:T(8,128)}), (f32[1,256,3072]{2,1,0:T(8,128)}, f32[1,256,1024]{2,1,0:T(8,128)}, ...) | async-done | bytes 12582928 | tf_op jit(solution)/shard_map/psum | solution.py:257
  (1224 shorter events, 877.2 us)
Async XLA Ops:
  7.2 47.9 %all-gather.11.cloned.1.call-start = ((), (), s32[]{:S(2)}) async-start(), calls=%async_computation.7 | async-start | bytes 2621440 | tf_op jit(solution)/shard_map/all_gather | solution.py:194
  7.9 161.5 %all-gather.9.cloned.1.call-start = ((), (), s32[]{:S(2)}) async-start(), calls=%async_computation.6 | async-start | bytes 7864320 | tf_op jit(solution)/shard_map/all_gather | solution.py:193
  8.7 463.6 %copy-start.26 = (f32[1,4096]{1,0:T(1,128)S(1)}, f32[1,4096]{1,0:T(1,128)}, u32[]{:S(2)}) copy-start(f32[1,4096]{1,0:T(1,128)} %param.29) | copy-start | bytes 49156
  8.7 463.5 %copy-start.54 = (f32[1,16]{1,0:T(1,128)S(1)}, f32[1,16]{1,0:T(1,128)}, u32[]{:S(2)}) copy-start(f32[1,16]{1,0:T(1,128)} %param.31) | copy-start | bytes 196
  8.7 463.5 %copy-start.58 = (s32[4,1]{0,1:T(1,128)S(1)}, s32[4,1]{0,1:T(1,128)}, u32[]{:S(2)}) copy-start(s32[4,1]{0,1:T(1,128)} %param.22) | copy-start | bytes 52
  8.7 310.2 %all-gather.13.cloned.1.call-start = ((), (), s32[]{:S(2)}) async-start(), calls=%async_computation.8 | async-start | bytes 10485760 | tf_op jit(solution)/shard_map/all_gather | solution.py:195
  9.4 458.8 %all-gather.15.cloned.1.call-start = ((), (), s32[]{:S(2)}) async-start(), calls=%async_computation.9 | async-start | bytes 10485760 | tf_op jit(solution)/shard_map/all_gather | solution.py:196
  55.1 417.1 %copy-start.6 = (bf16[1,1024,1024]{2,1,0:T(8,128)(2,1)S(1)}, bf16[1,1024,1024]{2,1,0:T(8,128)(2,1)}, u32[]{:S(2)}) copy-start(bf16[1,1024,1024]{2,1,0:T(8,128)(2,1)} %all-gather.11.cloned.1.call-done) | copy-start | bytes 6291460
  472.2 595.3 %copy-start.44 = (f32[4096]{0:T(1024)S(1)}, f32[4096]{0:T(1024)}, u32[]{:S(2)}) copy-start(f32[4096]{0:T(1024)} %custom-call.7) | copy-start | bytes 49156
  472.3 595.3 %copy-start.45 = (f32[4096]{0:T(1024)S(1)}, f32[4096]{0:T(1024)}, u32[]{:S(2)}) copy-start(f32[4096]{0:T(1024)} %custom-call.6) | copy-start | bytes 49156
  472.3 595.3 %copy-start.55 = (f32[16]{0:T(128)S(1)}, f32[16]{0:T(128)}, u32[]{:S(2)}) copy-start(f32[16]{0:T(128)} %custom-call.8) | copy-start | bytes 196
  472.3 50.4 %all-gather.19.cloned.1.call-start = ((), (), s32[]{:S(2)}) async-start(), calls=%async_computation.16 | async-start | bytes 2621440 | tf_op jit(solution)/shard_map/while/body/eval_jaxpr/all_gather | solution.py:56
  486.2 74.1 %all-gather.17.cloned.1.call-start = ((), (), s32[]{:S(2)}) async-start(), calls=%async_computation.15 | async-start | bytes 2621440 | tf_op jit(solution)/shard_map/while/body/eval_jaxpr/all_gather | solution.py:57
  588.0 3.3 collective-permute-start
  592.0 49.3 %all-gather.19.cloned.1.call-start = ((), (), s32[]{:S(2)}) async-start(), calls=%async_computation.16 | async-start | bytes 2621440 | tf_op jit(solution)/shard_map/while/body/eval_jaxpr/all_gather | solution.py:56
  605.8 73.3 %all-gather.17.cloned.1.call-start = ((), (), s32[]{:S(2)}) async-start(), calls=%async_computation.15 | async-start | bytes 2621440 | tf_op jit(solution)/shard_map/while/body/eval_jaxpr/all_gather | solution.py:57
  706.7 3.2 collective-permute-start
  710.8 49.3 %all-gather.19.cloned.1.call-start = ((), (), s32[]{:S(2)}) async-start(), calls=%async_computation.16 | async-start | bytes 2621440 | tf_op jit(solution)/shard_map/while/body/eval_jaxpr/all_gather | solution.py:56
  724.6 73.1 %all-gather.17.cloned.1.call-start = ((), (), s32[]{:S(2)}) async-start(), calls=%async_computation.15 | async-start | bytes 2621440 | tf_op jit(solution)/shard_map/while/body/eval_jaxpr/all_gather | solution.py:57
  825.4 3.2 collective-permute-start
  829.4 49.3 %all-gather.19.cloned.1.call-start = ((), (), s32[]{:S(2)}) async-start(), calls=%async_computation.16 | async-start | bytes 2621440 | tf_op jit(solution)/shard_map/while/body/eval_jaxpr/all_gather | solution.py:56
  843.2 73.1 %all-gather.17.cloned.1.call-start = ((), (), s32[]{:S(2)}) async-start(), calls=%async_computation.15 | async-start | bytes 2621440 | tf_op jit(solution)/shard_map/while/body/eval_jaxpr/all_gather | solution.py:57
  944.0 3.2 collective-permute-start
  948.0 49.3 %all-gather.19.cloned.1.call-start = ((), (), s32[]{:S(2)}) async-start(), calls=%async_computation.16 | async-start | bytes 2621440 | tf_op jit(solution)/shard_map/while/body/eval_jaxpr/all_gather | solution.py:56
  961.8 73.1 %all-gather.17.cloned.1.call-start = ((), (), s32[]{:S(2)}) async-start(), calls=%async_computation.15 | async-start | bytes 2621440 | tf_op jit(solution)/shard_map/while/body/eval_jaxpr/all_gather | solution.py:57
  1062.6 3.2 collective-permute-start
  1067.9 46.6 %all-gather.23.cloned.1.call-start = ((), (), s32[]{:S(2)}) async-start(), calls=%async_computation.18 | async-start | bytes 2621440 | tf_op jit(solution)/shard_map/while/body/eval_jaxpr/all_gather | solution.py:56
  1079.1 73.0 %all-gather.21.cloned.1.call-start = ((), (), s32[]{:S(2)}) async-start(), calls=%async_computation.17 | async-start | bytes 2621440 | tf_op jit(solution)/shard_map/while/body/eval_jaxpr/all_gather | solution.py:57
  1080.2 196.6 %reduce-scatter.15.cloned.1.call-start = ((), (), s32[]{:S(2)}) async-start(), calls=%async_computation.19 | async-start | bytes 5242880 | tf_op jit(solution)/shard_map/while/body/eval_jaxpr/reduce_scatter | solution.py:148
  1211.3 108.3 %reduce-scatter.17.cloned.1.call-start = ((), (), s32[]{:S(2)}) async-start(), calls=%async_computation.20 | async-start | bytes 5242880 | tf_op jit(solution)/shard_map/while/body/eval_jaxpr/reduce_scatter | solution.py:147
  1268.3 52.6 %copy-start.30 = (f32[1,1024]{1,0:T(1,128)S(1)}, f32[1,1024]{1,0:T(1,128)}, u32[]{:S(2)}) copy-start(f32[1,1024]{1,0:T(1,128)} %copy-done.29) | copy-start | bytes 12292 | tf_op jit(solution)/shard_map/while
  1268.3 52.6 %copy-start.41 = (f32[256]{0:T(256)S(1)}, f32[256]{0:T(256)}, u32[]{:S(2)}) copy-start(f32[256]{0:T(256)} %copy-done.40) | copy-start | bytes 3076 | tf_op jit(solution)/shard_map/while
  1329.0 9.4 collective-permute-start.1
  1339.5 47.3 %all-gather.23.cloned.1.call-start = ((), (), s32[]{:S(2)}) async-start(), calls=%async_computation.18 | async-start | bytes 2621440 | tf_op jit(solution)/shard_map/while/body/eval_jaxpr/all_gather | solution.py:56
  1350.7 73.7 %all-gather.21.cloned.1.call-start = ((), (), s32[]{:S(2)}) async-start(), calls=%async_computation.17 | async-start | bytes 2621440 | tf_op jit(solution)/shard_map/while/body/eval_jaxpr/all_gather | solution.py:57
  1351.8 207.8 %reduce-scatter.15.cloned.1.call-start = ((), (), s32[]{:S(2)}) async-start(), calls=%async_computation.19 | async-start | bytes 5242880 | tf_op jit(solution)/shard_map/while/body/eval_jaxpr/reduce_scatter | solution.py:148
  1483.7 108.5 %reduce-scatter.17.cloned.1.call-start = ((), (), s32[]{:S(2)}) async-start(), calls=%async_computation.20 | async-start | bytes 5242880 | tf_op jit(solution)/shard_map/while/body/eval_jaxpr/reduce_scatter | solution.py:147
  1548.3 45.1 %copy-start.30 = (f32[1,1024]{1,0:T(1,128)S(1)}, f32[1,1024]{1,0:T(1,128)}, u32[]{:S(2)}) copy-start(f32[1,1024]{1,0:T(1,128)} %copy-done.29) | copy-start | bytes 12292 | tf_op jit(solution)/shard_map/while
  1548.3 45.1 %copy-start.41 = (f32[256]{0:T(256)S(1)}, f32[256]{0:T(256)}, u32[]{:S(2)}) copy-start(f32[256]{0:T(256)} %copy-done.40) | copy-start | bytes 3076 | tf_op jit(solution)/shard_map/while
  1601.6 12.2 collective-permute-start.1
  1614.8 47.3 %all-gather.23.cloned.1.call-start = ((), (), s32[]{:S(2)}) async-start(), calls=%async_computation.18 | async-start | bytes 2621440 | tf_op jit(solution)/shard_map/while/body/eval_jaxpr/all_gather | solution.py:56
  1626.1 73.7 %all-gather.21.cloned.1.call-start = ((), (), s32[]{:S(2)}) async-start(), calls=%async_computation.17 | async-start | bytes 2621440 | tf_op jit(solution)/shard_map/while/body/eval_jaxpr/all_gather | solution.py:57
  1627.1 207.6 %reduce-scatter.15.cloned.1.call-start = ((), (), s32[]{:S(2)}) async-start(), calls=%async_computation.19 | async-start | bytes 5242880 | tf_op jit(solution)/shard_map/while/body/eval_jaxpr/reduce_scatter | solution.py:148
  1758.7 108.3 %reduce-scatter.17.cloned.1.call-start = ((), (), s32[]{:S(2)}) async-start(), calls=%async_computation.20 | async-start | bytes 5242880 | tf_op jit(solution)/shard_map/while/body/eval_jaxpr/reduce_scatter | solution.py:147
  1823.3 45.0 %copy-start.30 = (f32[1,1024]{1,0:T(1,128)S(1)}, f32[1,1024]{1,0:T(1,128)}, u32[]{:S(2)}) copy-start(f32[1,1024]{1,0:T(1,128)} %copy-done.29) | copy-start | bytes 12292 | tf_op jit(solution)/shard_map/while
  1823.3 45.0 %copy-start.41 = (f32[256]{0:T(256)S(1)}, f32[256]{0:T(256)}, u32[]{:S(2)}) copy-start(f32[256]{0:T(256)} %copy-done.40) | copy-start | bytes 3076 | tf_op jit(solution)/shard_map/while
  1876.5 12.2 collective-permute-start.1
  1890.0 47.3 %all-gather.23.cloned.1.call-start = ((), (), s32[]{:S(2)}) async-start(), calls=%async_computation.18 | async-start | bytes 2621440 | tf_op jit(solution)/shard_map/while/body/eval_jaxpr/all_gather | solution.py:56
  1901.2 73.8 %all-gather.21.cloned.1.call-start = ((), (), s32[]{:S(2)}) async-start(), calls=%async_computation.17 | async-start | bytes 2621440 | tf_op jit(solution)/shard_map/while/body/eval_jaxpr/all_gather | solution.py:57
  1902.2 207.9 %reduce-scatter.15.cloned.1.call-start = ((), (), s32[]{:S(2)}) async-start(), calls=%async_computation.19 | async-start | bytes 5242880 | tf_op jit(solution)/shard_map/while/body/eval_jaxpr/reduce_scatter | solution.py:148
  2034.2 108.3 %reduce-scatter.17.cloned.1.call-start = ((), (), s32[]{:S(2)}) async-start(), calls=%async_computation.20 | async-start | bytes 5242880 | tf_op jit(solution)/shard_map/while/body/eval_jaxpr/reduce_scatter | solution.py:147
  2151.9 12.2 collective-permute-start.1
  2165.2 47.3 %all-gather.23.cloned.1.call-start = ((), (), s32[]{:S(2)}) async-start(), calls=%async_computation.18 | async-start | bytes 2621440 | tf_op jit(solution)/shard_map/while/body/eval_jaxpr/all_gather | solution.py:56
  2176.4 73.9 %all-gather.21.cloned.1.call-start = ((), (), s32[]{:S(2)}) async-start(), calls=%async_computation.17 | async-start | bytes 2621440 | tf_op jit(solution)/shard_map/while/body/eval_jaxpr/all_gather | solution.py:57
  2177.5 207.9 %reduce-scatter.15.cloned.1.call-start = ((), (), s32[]{:S(2)}) async-start(), calls=%async_computation.19 | async-start | bytes 5242880 | tf_op jit(solution)/shard_map/while/body/eval_jaxpr/reduce_scatter | solution.py:148
  2309.4 108.5 %reduce-scatter.17.cloned.1.call-start = ((), (), s32[]{:S(2)}) async-start(), calls=%async_computation.20 | async-start | bytes 5242880 | tf_op jit(solution)/shard_map/while/body/eval_jaxpr/reduce_scatter | solution.py:147
  2374.1 45.1 %copy-start.30 = (f32[1,1024]{1,0:T(1,128)S(1)}, f32[1,1024]{1,0:T(1,128)}, u32[]{:S(2)}) copy-start(f32[1,1024]{1,0:T(1,128)} %copy-done.29) | copy-start | bytes 12292 | tf_op jit(solution)/shard_map/while
  2374.1 45.1 %copy-start.41 = (f32[256]{0:T(256)S(1)}, f32[256]{0:T(256)}, u32[]{:S(2)}) copy-start(f32[256]{0:T(256)} %copy-done.40) | copy-start | bytes 3076 | tf_op jit(solution)/shard_map/while
  2427.3 12.2 collective-permute-start.1
  2442.2 81.3 %reduce-scatter.9.cloned.1.call-start = ((), (), s32[]{:S(2)}) async-start(), calls=%async_computation.11 | async-start | bytes 5242880 | tf_op jit(solution)/shard_map/reduce_scatter | solution.py:253
  2442.9 295.3 %reduce-scatter.7.cloned.1.call-start = ((), (), s32[]{:S(2)}) async-start(), calls=%async_computation.10 | async-start | bytes 15728640 | tf_op jit(solution)/shard_map/reduce_scatter | solution.py:252
  2443.5 575.2 %reduce-scatter.11.cloned.1.call-start = ((), (), s32[]{:S(2)}) async-start(), calls=%async_computation.12 | async-start | bytes 20971520 | tf_op jit(solution)/shard_map/reduce_scatter | solution.py:254
  2444.1 858.1 %reduce-scatter.13.cloned.1.call-start = ((), (), s32[]{:S(2)}) async-start(), calls=%async_computation.13 | async-start | bytes 20971520 | tf_op jit(solution)/shard_map/reduce_scatter | solution.py:255
  2444.9 1108.2 %all-reduce.4.cloned.1.call-start = ((), (), s32[]{:S(2)}) async-start(), calls=%async_computation.14 | async-start | bytes 25165824 | tf_op jit(solution)/shard_map/psum | solution.py:257
  (284 other events, 2354.5 us)
Sparse Core Ops, SparseCore 0:
  9.6 45.4 all-gather.10
  56.7 112.6 all-gather.8
  171.0 147.8 all-gather.12
  320.3 147.8 all-gather.14
  486.3 36.3 all-gather.18
  525.1 35.1 all-gather.16
  605.9 35.3 all-gather.18
  643.9 35.1 all-gather.16
  724.7 35.3 all-gather.18
  762.5 35.1 all-gather.16
  843.3 35.3 all-gather.18
  881.1 35.1 all-gather.16
  962.0 35.3 all-gather.18
  999.7 35.1 all-gather.16
  1079.3 35.1 all-gather.22
  1116.9 35.1 all-gather.20
  1211.4 52.6 reduce-scatter.14
  1266.9 52.6 reduce-scatter.16
  1350.9 35.9 all-gather.22
  1389.3 35.1 all-gather.20
  1483.8 52.6 reduce-scatter.14
  1539.4 52.6 reduce-scatter.16
  1626.2 35.9 all-gather.22
  1664.6 35.1 all-gather.20
  1758.8 52.6 reduce-scatter.14
  1814.3 52.6 reduce-scatter.16
  1901.3 35.9 all-gather.22
  1939.8 35.1 all-gather.20
  2034.3 52.6 reduce-scatter.14
  2089.8 52.6 reduce-scatter.16
  2176.5 35.9 all-gather.22
  2215.0 35.1 all-gather.20
  2309.5 52.6 reduce-scatter.14
  2365.2 52.6 reduce-scatter.16
  2445.9 77.5 reduce-scatter.8
  2525.8 212.3 reduce-scatter.6
  2740.5 278.1 reduce-scatter.10
  3021.1 281.0 reduce-scatter.12
  3306.4 246.5 all-reduce.3
where the time goes:
time: 3580 us; the launch traced here: 3570 us
  waiting for transfers between devices  2240 us (63%)
  matrix products  786 us (22%)
  other arithmetic  278 us (8%)
  local copies, waits for them, and re-layouts  151 us (4%)
  blocking collectives  76.8 us (2%)
    all_gather x10, waiting for transfers between devices, forward_parts(): lax.all_gather(key_rows, 'dp', axis=0, tiled=True)  303 us
    reduce_scatter x1, waiting for transfers between devices, local(): lax.psum_scatter(big_sums[3][None], 'shard', scatter_dimension=1, tiled=T...  283 us
    reduce_scatter x1, waiting for transfers between devices, local(): lax.psum_scatter(big_sums[2][None], 'shard', scatter_dimension=1, tiled=T...  281 us
    all_gather x10, waiting for transfers between devices, forward_parts(): lax.all_gather(value_rows, 'dp', axis=0, tiled=True)  269 us
    reduce_scatter x1, waiting for transfers between devices, local(): lax.psum_scatter(big_sums[0][None], 'shard', scatter_dimension=1, tiled=T...  215 us
    dot_general x20, matrix products, contract_rows(): lax.dot_general(left, right, (((0,), (0,)), ((), ())), preferred_element_...  199 us
    psum x1, waiting for transfers between devices, local(): shares = lax.psum((shares[0], shares[1], shares[2], shares[3]), 'dp')  173 us
    reduce_scatter x5, waiting for transfers between devices, backward_parts(): lax.psum_scatter(full_keys, 'dp', scatter_dimension=0, tiled=True)  166 us
  transfers between devices with their start and end apart: 49, of which 39 were waited for; matrix products, arithmetic and copies ran while one was open for 15% of the time, Pallas kernels for 0%

commit v1 on v0

--- a/solution.py
+++ b/solution.py
@@ -3,6 +3,8 @@
 import jax
 import jax.numpy as jnp
 from jax import lax
+from jax.experimental import pallas as pl
+from jax.experimental.pallas import tpu as pltpu
 from jax.sharding import PartitionSpec as P
 
 EPSILON = 1e-05
@@ -175,7 +177,7 @@
     return first_term + second_term
 
 
-def local(
+def general(
     boundary,
     first_len,
     qkv_weight,
@@ -272,6 +274,1049 @@
     )
 
 
+def core_swap(value):
+    return lax.ppermute(value, "section", [(0, 1), (1, 0)])
+
+
+def pick(value, index):
+    return lax.dynamic_index_in_dim(value, index, 0, keepdims=False)
+
+
+BF16 = jnp.bfloat16
+F32 = jnp.float32
+TILE = 256
+VMEM_BYTES = 56 * 2**20
+
+
+def rows_spec(columns):
+    return pl.BlockSpec((TILE, columns), lambda step: (step, 0))
+
+
+def group_spec(columns):
+    return pl.BlockSpec((4, TILE, columns), lambda step: (0, step, 0))
+
+
+def fixed_spec(shape):
+    return pl.BlockSpec(shape, lambda step: (0,) * len(shape))
+
+
+def call_rows(kernel, out_shapes, out_specs, in_specs, flops, moved):
+    return pl.pallas_call(
+        kernel,
+        grid=(4,),
+        in_specs=in_specs,
+        out_specs=out_specs,
+        out_shape=out_shapes,
+        compiler_params=pltpu.CompilerParams(vmem_limit_bytes=VMEM_BYTES),
+        cost_estimate=pl.CostEstimate(flops=flops, bytes_accessed=moved, transcendentals=0),
+    )
+
+
+def array(shape, dtype):
+    return jax.ShapeDtypeStruct(shape, dtype)
+
+
+def dot(left, right):
+    return jnp.dot(left, right, preferred_element_type=F32)
+
+
+def dot_nt(left, right):
+    return lax.dot_general(left, right, (((1,), (1,)), ((), ())), preferred_element_type=F32)
+
+
+def standard(values_in):
+    centre = values_in - jnp.mean(values_in, axis=-1, keepdims=True)
+    spread_of = jnp.mean(centre * centre, axis=-1, keepdims=True)
+    scale = lax.rsqrt(spread_of + EPSILON)
+    return centre * scale, scale
+
+
+def standard_back(unit_values, scale, gain, grad):
+    inner = grad * gain
+    first = jnp.mean(inner, axis=-1, keepdims=True)
+    second = jnp.mean(inner * unit_values, axis=-1, keepdims=True)
+    back = scale * (inner - first - unit_values * second)
+    return back, jnp.sum(grad * unit_values, axis=0, keepdims=True), jnp.sum(grad, axis=0, keepdims=True)
+
+
+def add_rows(ref, row, value):
+    ref[row : row + 1, :] += value
+
+
+def clear_first(*refs):
+    @pl.when(pl.program_id(0) == 0)
+    def unused():
+        for ref in refs:
+            ref[...] = jnp.zeros_like(ref)
+
+
+def project(entry, gain, shift, weight):
+    def kernel(x_ref, gain_ref, shift_ref, w_ref, normed_ref, proj_ref):
+        unit_x, unused = standard(x_ref[...].astype(F32))
+        normed = (unit_x * gain_ref[...] + shift_ref[...]).astype(BF16)
+        normed_ref[...] = normed
+        for group in range(4):
+            proj_ref[group] = dot(normed, w_ref[group]).astype(BF16)
+
+    return call_rows(
+        kernel,
+        (array((1024, 1024), BF16), array((4, 1024, 384), BF16)),
+        (rows_spec(1024), group_spec(384)),
+        [rows_spec(1024), fixed_spec((1, 1024)), fixed_spec((1, 1024)), fixed_spec((4, 1024, 384))],
+        2 * 1024 * 1024 * 1536,
+        10 * 2**20,
+    )(entry, gain, shift, weight)
+
+
+def project_next(residual, part_own, part_other, gain, shift, weight):
+    def kernel(res_ref, a_ref, b_ref, gain_ref, shift_ref, w_ref, entry_ref, normed_ref, proj_ref):
+        entry = (res_ref[...] + (a_ref[...].astype(F32) + b_ref[...].astype(F32))).astype(BF16)
+        entry_ref[...] = entry
+        unit_x, unused = standard(entry.astype(F32))
+        normed = (unit_x * gain_ref[...] + shift_ref[...]).astype(BF16)
+        normed_ref[...] = normed
+        for group in range(4):
+            proj_ref[group] = dot(normed, w_ref[group]).astype(BF16)
+
+    return call_rows(
+        kernel,
+        (array((1024, 1024), BF16), array((1024, 1024), BF16), array((4, 1024, 384), BF16)),
+        (rows_spec(1024), rows_spec(1024), group_spec(384)),
+        [rows_spec(1024)] * 3
+        + [fixed_spec((1, 1024)), fixed_spec((1, 1024)), fixed_spec((4, 1024, 384))],
+        2 * 1024 * 1024 * 1536,
+        18 * 2**20,
+    )(residual, part_own, part_other, gain, shift, weight)
+
+
+def lane_masks(rows):
+    lanes = lax.broadcasted_iota(jnp.int32, (rows, 128), 1)
+    return lanes < 64
+
+
+def fill_bias(bias_ref, split_at):
+    @pl.when(pl.program_id(0) == 0)
+    def unused():
+        for block in range(4):
+            keys = lax.broadcasted_iota(jnp.int32, (256, 1024), 0) + block * 256
+            queries = lax.broadcasted_iota(jnp.int32, (256, 1024), 1)
+            allowed = ((queries < split_at) == (keys < split_at)) & (keys <= queries)
+            bias_ref[pl.ds(block * 256, 256), :] = jnp.where(allowed, 0.0, -1e30)
+
+
+def attend_kernel(split_ref, q_ref, k_ref, v_ref, scale_ref, out_ref, scaled_ref, log_ref, bias_ref, turned_ref):
+    fill_bias(bias_ref, split_ref[0])
+    turned_ref[...] = v_ref[0].astype(F32).T.astype(BF16)
+    low_lanes = lane_masks(256)
+    for block in range(4):
+        seen = (block + 1) * 256
+        span = pl.ds(block * 256, 256)
+        q = q_ref[0, span, :] * 0.125
+        keys = k_ref[0, pl.ds(0, seen), :]
+        halves_out = []
+        for half in range(2):
+            q_half = jnp.where(low_lanes if half == 0 else ~low_lanes, q, 0.0).astype(BF16)
+            scores = dot_nt(keys, q_half) + bias_ref[pl.ds(0, seen), span]
+            top = jnp.max(scores, axis=0, keepdims=True)
+            powers = jnp.exp(scores - top)
+            total = jnp.sum(powers, axis=0, keepdims=True)
+            log_ref[0, half : half + 1, span] = top + jnp.log(total)
+            mixed = dot(turned_ref[half * 64 : half * 64 + 64, :seen], powers.astype(BF16))
+            halves_out.append(mixed * (1.0 / total))
+        head_out = jnp.concatenate(halves_out, axis=0).T
+        out_ref[span, :] = head_out.astype(BF16)
+        scaled_ref[span, :] = (head_out * scale_ref[0]).astype(BF16)
+
+
+def attention(proj, split_at, scale_rows):
+    def cut(third):
+        return pl.BlockSpec((1, 1024, 128), lambda group, split: (group, 0, third))
+
+    return pl.pallas_call(
+        attend_kernel,
+        grid_spec=pltpu.PrefetchScalarGridSpec(
+            num_scalar_prefetch=1,
+            grid=(4,),
+            in_specs=[cut(0), cut(1), cut(2), pl.BlockSpec((1, 1, 128), lambda group, split: (group, 0, 0))],
+            out_specs=[
+                pl.BlockSpec((1024, 128), lambda group, split: (0, group)),
+                pl.BlockSpec((1024, 128), lambda group, split: (0, group)),
+                pl.BlockSpec((1, 2, 1024), lambda group, split: (group, 0, 0)),
+            ],
+            scratch_shapes=[pltpu.VMEM((1024, 1024), F32), pltpu.VMEM((128, 1024), BF16)],
+        ),
+        out_shape=(array((1024, 512), BF16), array((1024, 512), BF16), array((4, 2, 1024), F32)),
+        compiler_params=pltpu.CompilerParams(vmem_limit_bytes=VMEM_BYTES),
+        cost_estimate=pl.CostEstimate(flops=20 * 10**9, bytes_accessed=8 * 2**20, transcendentals=0),
+    )(split_at, proj, proj, proj, scale_rows)
+
+
+def attend_back_kernel(
+    split_ref, q_ref, k_ref, v_ref, grad_ref, out_ref, log_ref, back_ref, bias_ref, turned_ref, dk_ref, dv_ref
+):
+    fill_bias(bias_ref, split_ref[0])
+    turned_ref[...] = k_ref[0].astype(F32).T.astype(BF16)
+    dk_ref[...] = jnp.zeros_like(dk_ref)
+    dv_ref[...] = jnp.zeros_like(dv_ref)
+    low_lanes = lane_masks(256)
+    for block in range(4):
+        seen = (block + 1) * 256
+        span = pl.ds(block * 256, 256)
+        q = q_ref[0, span, :] * 0.125
+        grad = grad_ref[span, :]
+        product = (grad.astype(F32) * out_ref[span, :].astype(F32)).T
+        keys = k_ref[0, pl.ds(0, seen), :]
+        values = v_ref[0, pl.ds(0, seen), :]
+        dq_halves, lows, d_scores_all, q_halves, grad_halves = [], [], [], [], []
+        for half in range(2):
+            mask = low_lanes if half == 0 else ~low_lanes
+            q_half = jnp.where(mask, q, 0.0).astype(BF16)
+            grad_half = jnp.where(mask, grad, 0.0).astype(BF16)
+            row_dot = jnp.sum(product[half * 64 : half * 64 + 64, :], axis=0, keepdims=True)
+            scores = dot_nt(keys, q_half) + bias_ref[pl.ds(0, seen), span]
+            attend = jnp.exp(scores - log_ref[0, half : half + 1, span])
+            d_attend = dot_nt(values, grad_half)
+            d_scores = (attend * (d_attend - row_dot)).astype(BF16)
+            dq_halves.append(dot(turned_ref[half * 64 : half * 64 + 64, :seen], d_scores))
+            lows.append(attend.astype(BF16))
+            d_scores_all.append(d_scores)
+            q_halves.append(q_half)
+            grad_halves.append(grad_half)
+        dv_ref[pl.ds(0, seen), :] += dot(jnp.concatenate(lows, axis=1), jnp.concatenate(grad_halves, axis=0))
+        dk_ref[pl.ds(0, seen), :] += dot(jnp.concatenate(d_scores_all, axis=1), jnp.concatenate(q_halves, axis=0))
+        back_ref[0, span, 0:128] = (jnp.concatenate(dq_halves, axis=0).T * 0.125).astype(BF16)
+    back_ref[0, :, 128:256] = dk_ref[...].astype(BF16)
+    back_ref[0, :, 256:384] = dv_ref[...].astype(BF16)
+
+
+def attention_back(proj, split_at, grad, head_out, logs):
+    def cut(third):
+        return pl.BlockSpec((1, 1024, 128), lambda group, split: (group, 0, third))
+
+    columns = pl.BlockSpec((1024, 128), lambda group, split: (0, group))
+    return pl.pallas_call(
+        attend_back_kernel,
+        grid_spec=pltpu.PrefetchScalarGridSpec(
+            num_scalar_prefetch=1,
+            grid=(4,),
+            in_specs=[cut(0), cut(1), cut(2), columns, columns, pl.BlockSpec((1, 2, 1024), lambda group, split: (group, 0, 0))],
+            out_specs=pl.BlockSpec((1, 1024, 384), lambda group, split: (group, 0, 0)),
+            scratch_shapes=[
+                pltpu.VMEM((1024, 1024), F32),
+                pltpu.VMEM((128, 1024), BF16),
+                pltpu.VMEM((1024, 128), F32),
+                pltpu.VMEM((1024, 128), F32),
+            ],
+        ),
+        out_shape=array((4, 1024, 384), BF16),
+        compiler_params=pltpu.CompilerParams(vmem_limit_bytes=VMEM_BYTES),
+        cost_estimate=pl.CostEstimate(flops=40 * 10**9, bytes_accessed=10 * 2**20, transcendentals=0),
+    )(split_at, proj, proj, proj, grad, head_out, logs)
+
+
+def two_columns(first, second):
+    return jnp.where(lane_masks(first.shape[0]), first, second)
+
+
+def widen(entry, part_own, part_other, gains, shifts, weight):
+    def kernel(x_ref, a_ref, b_ref, gain_ref, shift_ref, w_ref, res_ref, ffn_ref, gelu_ref, slope_ref, stat_ref):
+        branch = a_ref[...].astype(F32) + b_ref[...].astype(F32)
+        unit_b, unused = standard(branch)
+        residual = x_ref[...].astype(F32) + unit_b * gain_ref[1:2] + shift_ref[1:2]
+        res_ref[...] = residual
+        unit_r, unused = standard(residual)
+        ffn_input = (unit_r * gain_ref[2:3] + shift_ref[2:3]).astype(BF16)
+        ffn_ref[...] = ffn_input
+        first, second = [], []
+        for group in range(4):
+            hidden = dot(ffn_input, w_ref[group])
+            half = 0.5 + 0.5 * lax.erf(hidden * math.sqrt(0.5))
+            gelu = hidden * half
+            bell = jnp.exp(-0.5 * hidden * hidden) * (1.0 / math.sqrt(2.0 * math.pi))
+            gelu_ref[group] = gelu.astype(BF16)
+            slope_ref[group] = (half + hidden * bell).astype(BF16)
+            mean = jnp.mean(gelu, axis=-1, keepdims=True)
+            centre = gelu - mean
+            first.append(mean)
+            second.append(jnp.mean(centre * centre, axis=-1, keepdims=True))
+        mean = 0.25 * (first[0] + first[1] + first[2] + first[3])
+        spread_of = sum(0.25 * (s + (m - mean) * (m - mean)) for m, s in zip(first, second))
+        stat_ref[...] = two_columns(mean, spread_of)
+
+    wide = array((4, 1024, 512), BF16)
+    return call_rows(
+        kernel,
+        (array((1024, 1024), F32), array((1024, 1024), BF16), wide, wide, array((1024, 128), F32)),
+        (rows_spec(1024), rows_spec(1024), group_spec(512), group_spec(512), rows_spec(128)),
+        [rows_spec(1024)] * 3 + [fixed_spec((3, 1024)), fixed_spec((3, 1024)), fixed_spec((4, 1024, 512))],
+        2 * 1024 * 1024 * 2048,
+        30 * 2**20,
+    )(entry, part_own, part_other, gains, shifts, weight)
+
+
+def mid_stats(own, other):
+    mean_own, mean_other = own[:, 0:1], other[:, 0:1]
+    gap = mean_own - mean_other
+    spread_of = 0.5 * (own[:, 64:65] + other[:, 64:65]) + 0.25 * gap * gap
+    return 0.5 * (mean_own + mean_other), lax.rsqrt(spread_of + EPSILON)
+
+
+def narrow(gelu, own, other, gain, shift, weight):
+    def kernel(g_ref, own_ref, other_ref, gain_ref, shift_ref, w_ref, mid_ref, part_ref):
+        mean, scale = mid_stats(own_ref[...], other_ref[...])
+        total = jnp.zeros((TILE, 1024), F32)
+        for group in range(4):
+            unit_m = (g_ref[group].astype(F32) - mean) * scale
+            middle = (unit_m * gain_ref[group : group + 1] + shift_ref[group : group + 1]).astype(BF16)
+            mid_ref[group] = middle
+            total = total + dot(middle, w_ref[group])
+        part_ref[...] = total.astype(BF16)
+
+    return call_rows(
+        kernel,
+        (array((4, 1024, 512), BF16), array((1024, 1024), BF16)),
+        (group_spec(512), rows_spec(1024)),
+        [group_spec(512), rows_spec(128), rows_spec(128), fixed_spec((4, 512)), fixed_spec((4, 512)), fixed_spec((4, 512, 1024))],
+        2 * 1024 * 1024 * 2048,
+        15 * 2**20,
+    )(gelu, own, other, gain, shift, weight)
+
+
+def narrow_back(grad, gelu, own, other, gain, weight):
+    def kernel(c_ref, g_ref, own_ref, other_ref, gain_ref, w_ref, dm_ref, stat_ref, gg_ref, gs_ref):
+        clear_first(gg_ref, gs_ref)
+        mean, scale = mid_stats(own_ref[...], other_ref[...])
+        grad_low = c_ref[...]
+        first = jnp.zeros((TILE, 1), F32)
+        second = jnp.zeros((TILE, 1), F32)
+        for group in range(4):
+            d_middle = dot_nt(grad_low, w_ref[group])
+            dm_ref[group] = d_middle.astype(BF16)
+            unit_m = (g_ref[group].astype(F32) - mean) * scale
+            product = d_middle * unit_m
+            add_rows(gg_ref, group, jnp.sum(product, axis=0, keepdims=True))
+            add_rows(gs_ref, group, jnp.sum(d_middle, axis=0, keepdims=True))
+            row_gain = gain_ref[group : group + 1]
+            first = first + jnp.sum(d_middle * row_gain, axis=-1, keepdims=True)
+            second = second + jnp.sum(product * row_gain, axis=-1, keepdims=True)
+        stat_ref[...] = two_columns(first, second)
+
+    return call_rows(
+        kernel,
+        (array((4, 1024, 512), BF16), array((1024, 128), F32), array((4, 512), F32), array((4, 512), F32)),
+        (group_spec(512), rows_spec(128), fixed_spec((4, 512)), fixed_spec((4, 512))),
+        [rows_spec(1024), group_spec(512), rows_spec(128), rows_spec(128), fixed_spec((4, 512)), fixed_spec((4, 512, 1024))],
+        2 * 1024 * 1024 * 2048,
+        15 * 2**20,
+    )(grad, gelu, own, other, gain, weight)
+
+
+def widen_back(d_middle, gelu, slope, own, other, sum_own, sum_other, gain, weight):
+    def kernel(dm_ref, g_ref, s_ref, own_ref, other_ref, a_ref, b_ref, gain_ref, w_ref, dh_ref, part_ref):
+        mean, scale = mid_stats(own_ref[...], other_ref[...])
+        sums = (a_ref[...] + b_ref[...]) * (1.0 / 4096)
+        first, second = sums[:, 0:1], sums[:, 64:65]
+        total = jnp.zeros((TILE, 1024), F32)
+        for group in range(4):
+            unit_m = (g_ref[group].astype(F32) - mean) * scale
+            inner = dm_ref[group].astype(F32) * gain_ref[group : group + 1]
+            d_gelu = scale * (inner - first - unit_m * second)
+            d_hidden = (d_gelu * s_ref[group].astype(F32)).astype(BF16)
+            dh_ref[group] = d_hidden
+            total = total + dot_nt(d_hidden, w_ref[group])
+        part_ref[...] = total.astype(BF16)
+
+    return call_rows(
+        kernel,
+        (array((4, 1024, 512), BF16), array((1024, 1024), BF16)),
+        (group_spec(512), rows_spec(1024)),
+        [group_spec(512)] * 3 + [rows_spec(128)] * 4 + [fixed_spec((4, 512)), fixed_spec((4, 1024, 512))],
+        2 * 1024 * 1024 * 2048,
+        20 * 2**20,
+    )(d_middle, gelu, slope, own, other, sum_own, sum_other, gain, weight)
+
+
+def norms_back(grad, residual, d_own, d_other, b_own, b_other, gains, head_out, scale_row, weight):
+    def kernel(c_ref, res_ref, da_ref, db_ref, ba_ref, bb_ref, gain_ref, ho_ref, hs_ref, w_ref,
+               dr_ref, dbr_ref, dh_ref, sum_ref, head_ref):
+        clear_first(sum_ref, head_ref)
+        unit_r, scale_r = standard(res_ref[...])
+        d_ffn = da_ref[...].astype(F32) + db_ref[...].astype(F32)
+        back, gain_third, shift_third = standard_back(unit_r, scale_r, gain_ref[2:3], d_ffn)
+        d_residual = c_ref[...].astype(F32) + back
+        dr_ref[...] = d_residual
+        unit_b, scale_b = standard(ba_ref[...].astype(F32) + bb_ref[...].astype(F32))
+        back, gain_second, shift_second = standard_back(unit_b, scale_b, gain_ref[1:2], d_residual)
+        d_branch = back.astype(BF16)
+        dbr_ref[...] = d_branch
+        d_scaled = dot_nt(d_branch, w_ref[...])
+        dh_ref[...] = (d_scaled * hs_ref[...]).astype(BF16)
+        add_rows(head_ref, 0, jnp.sum(d_scaled * ho_ref[...].astype(F32), axis=0, keepdims=True))
+        for row, value in enumerate((gain_second, gain_third, shift_second, shift_third)):
+            add_rows(sum_ref, row, value)
+
+    return call_rows(
+        kernel,
+        (
+            array((1024, 1024), F32),
+            array((1024, 1024), BF16),
+            array((1024, 512), BF16),
+            array((8, 1024), F32),
+            array((8, 512), F32),
+        ),
+        (rows_spec(1024), rows_spec(1024), rows_spec(512), fixed_spec((8, 1024)), fixed_spec((8, 512))),
+        [rows_spec(1024)] * 6
+        + [fixed_spec((3, 1024)), rows_spec(512), fixed_spec((1, 512)), fixed_spec((512, 1024))],
+        2 * 1024 * 1024 * 512,
+        25 * 2**20,
+    )(grad, residual, d_own, d_other, b_own, b_other, gains, head_out, scale_row, weight)
+
+
+def project_back(d_proj, weight):
+    def kernel(d_ref, w_ref, part_ref):
+        total = dot_nt(d_ref[0], w_ref[0])
+        for group in range(1, 4):
+            total = total + dot_nt(d_ref[group], w_ref[group])
+        part_ref[...] = total.astype(BF16)
+
+    return call_rows(
+        kernel,
+        array((1024, 1024), BF16),
+        rows_spec(1024),
+        [group_spec(384), fixed_spec((4, 1024, 384))],
+        2 * 1024 * 1024 * 1536,
+        10 * 2**20,
+    )(d_proj, weight)
+
+
+def entry_back(d_residual, d_own, d_other, entry, gain):
+    def kernel(dr_ref, a_ref, b_ref, x_ref, gain_ref, dx_ref, sum_ref):
+        clear_first(sum_ref)
+        unit_x, scale_x = standard(x_ref[...].astype(F32))
+        d_normed = a_ref[...].astype(F32) + b_ref[...].astype(F32)
+        back, gain_first, shift_first = standard_back(unit_x, scale_x, gain_ref[...], d_normed)
+        dx_ref[...] = (dr_ref[...] + back).astype(BF16)
+        add_rows(sum_ref, 0, gain_first)
+        add_rows(sum_ref, 1, shift_first)
+
+    return call_rows(
+        kernel,
+        (array((1024, 1024), BF16), array((8, 1024), F32)),
+        (rows_spec(1024), fixed_spec((8, 1024))),
+        [rows_spec(1024)] * 4 + [fixed_spec((1, 1024))],
+        20 * 2**20,
+        15 * 2**20,
+    )(d_residual, d_own, d_other, entry, gain)
+
+
+def contract(left, right):
+    return lax.dot_general(left, right, (((0,), (0,)), ((), ())), preferred_element_type=F32)
+
+
+def layer_forward(projected, entry, weights, small, split_at):
+    normed, proj = projected
+    w_qkv, w_out, w_up, w_down = weights
+    gains, shifts, mid_gain, mid_shift, head_scale = small
+    scale_row = jnp.repeat(head_scale.reshape(8), 64)
+    head_out, scaled, logs = attention(proj, split_at, scale_row.reshape(4, 1, 128))
+    branch = dot(scaled, w_out).astype(BF16)
+    branch_other = core_swap(branch)
+    residual, ffn_input, gelu, slope, stat = widen(entry, branch, branch_other, gains, shifts, w_up)
+    stat_other = core_swap(stat)
+    middle, part = narrow(gelu, stat, stat_other, mid_gain, mid_shift, w_down)
+    part_other = core_swap(part)
+    kept = dict(
+        entry=entry, normed=normed, proj=proj, head_out=head_out, scaled=scaled, logs=logs, branch=branch,
+        branch_other=branch_other, residual=residual, ffn_input=ffn_input, gelu=gelu, slope=slope, stat=stat,
+        stat_other=stat_other, middle=middle, scale_row=scale_row, split_at=split_at,
+    )
+    return residual, part, part_other, kept
+
+
+def layer_backward(grad_low, weights, small, kept):
+    w_qkv, w_out, w_up, w_down = weights
+    gains, shifts, mid_gain, mid_shift, head_scale = small
+    middle, ffn_input, normed = kept["middle"], kept["ffn_input"], kept["normed"]
+    grad_down = jnp.einsum("pmk,mn->pkn", middle, grad_low, preferred_element_type=F32)
+    grad_down = grad_down.astype(BF16)
+    stat, stat_other = kept["stat"], kept["stat_other"]
+    d_middle, sums, g_mid_gain, g_mid_shift = narrow_back(
+        grad_low, kept["gelu"], stat, stat_other, mid_gain, w_down
+    )
+    sums_other = core_swap(sums)
+    d_hidden, part = widen_back(
+        d_middle, kept["gelu"], kept["slope"], stat, stat_other, sums, sums_other, mid_gain, w_up
+    )
+    part_other = core_swap(part)
+    grad_up = jnp.einsum("mk,pmn->pkn", ffn_input, d_hidden, preferred_element_type=F32)
+    grad_up = grad_up.astype(BF16).reshape(4, 4, 256, 512)
+    d_residual, d_branch, d_heads, norm_sums, head_sums = norms_back(
+        grad_low, kept["residual"], part, part_other, kept["branch"], kept["branch_other"], gains,
+        kept["head_out"], kept["scale_row"].reshape(1, 512), w_out,
+    )
+    grad_out = contract(kept["scaled"], d_branch)
+    grad_out = grad_out.astype(BF16).reshape(4, 128, 1024)
+    d_proj = attention_back(kept["proj"], kept["split_at"], d_heads, kept["head_out"], kept["logs"])
+    d_part = project_back(d_proj, w_qkv)
+    d_part_other = core_swap(d_part)
+    grad_qkv = jnp.einsum("mk,pmn->pkn", normed, d_proj, preferred_element_type=F32)
+    grad_qkv = grad_qkv.astype(BF16).reshape(4, 4, 256, 384)
+    d_x, first_sums = entry_back(d_residual, d_part, d_part_other, kept["entry"], gains[0:1])
+    return d_x, (grad_qkv, grad_out, grad_up, grad_down), (first_sums, norm_sums, g_mid_gain, g_mid_shift, head_sums)
+
+
+MESH = pl.DeviceIdType.MESH
+SIZES = ((256, 384), (128, 256), (256, 512), (512, 256))
+
+
+def partner(place, step):
+    return {0: place, 1: place + 1 - 2 * lax.rem(place, 2), 2: lax.rem(place + 2, 4), 3: 3 - place}[step]
+
+
+def here():
+    return lax.axis_index("section"), lax.axis_index("dp"), lax.axis_index("shard")
+
+
+def greet(core, place, depth):
+    barrier = pltpu.get_barrier_semaphore()
+    targets = [{"shard": lax.rem(depth + step, 4)} for step in (1, 2, 3)]
+    targets += [{"section": 1 - core, "shard": lax.rem(depth + step, 4)} for step in range(4)]
+    targets += [{"dp": partner(place, step)} for step in (1, 2, 3)]
+    for target in targets:
+        pl.semaphore_signal(barrier, inc=1, device_id=target, device_id_type=MESH)
+    pl.semaphore_wait(barrier, len(targets))
+
+
+def send(source, target, send_sem, recv_sem, device):
+    copy = pltpu.make_async_remote_copy(
+        src_ref=source, dst_ref=target, send_sem=send_sem, recv_sem=recv_sem,
+        device_id=device, device_id_type=MESH,
+    )
+    copy.start()
+
+
+def await_bytes(view, sem):
+    pltpu.make_async_copy(view, view, sem).wait()
+
+
+def lanes(start, size):
+    return pl.ds(pl.multiple_of(start, 128), size)
+
+
+def raw_views(raw, matrix, half, quarter):
+    if matrix == 0:
+        return [raw[0].at[:, lanes(third * 1024 + quarter * 256 + half * 128, 128)] for third in range(3)]
+    if matrix == 1:
+        return [raw[1].at[pl.ds(half * 128, 128), lanes(quarter * 256, 256)]]
+    if matrix == 2:
+        return [raw[2].at[:, lanes(quarter * 1024 + half * 512, 512)]]
+    return [raw[3].at[pl.ds(half * 512, 512), lanes(quarter * 256, 256)]]
+
+
+def whole_view(whole, matrix, quarter, shard):
+    if matrix in (0, 2):
+        return whole[matrix].at[quarter, shard]
+    return whole[matrix].at[shard, :, lanes(quarter * 256, 256)]
+
+
+def whole_views(whole, matrix, quarter, shard):
+    if matrix == 0:
+        return [whole[0].at[quarter, shard, :, pl.ds(third * 128, 128)] for third in range(3)]
+    return [whole_view(whole, matrix, quarter, shard)]
+
+
+def pieces_view(whole, matrix, first, second):
+    if matrix in (0, 2):
+        return whole[matrix].at[pl.ds(0, first), pl.ds(0, second)]
+    return whole[matrix].at[pl.ds(0, first), :, pl.ds(0, 256 * second)]
+
+
+def gather_kernel(
+    items, qkv, out, up, down, gains, shifts, mid_gain, mid_shift, heads,
+    entry, cotangent, wq0, wo0, wu0, wd0, wq1, wo1, wu1, wd1, gains2, shifts2, mid_gain2, mid_shift2, heads2,
+    item_send, item_recv, item_pass, own_send, own_recv, deep_send, deep_recv, hop_send, hop_recv, small_sems,
+):
+    core, place, depth = here()
+    raw = (qkv, out, up, down)
+    wholes = ((wq0, wo0, wu0, wd0), (wq1, wo1, wu1, wd1))
+    arrays = (entry, cotangent)
+    smalls = ((gains, gains2), (shifts, shifts2), (mid_gain, mid_gain2), (mid_shift, mid_shift2), (heads, heads2))
+    greet(core, place, depth)
+
+    for layer in (0, 1):
+        @pl.when(core == layer)
+        def unused():
+            for step in (1, 2, 3):
+                send(items.at[partner(place, step)], arrays[layer].at[place], item_send.at[layer, step],
+                     item_recv.at[layer, step], {"dp": partner(place, step)})
+            pltpu.make_async_copy(items.at[place], arrays[layer].at[place], item_send.at[layer, 0]).start()
+            send(items.at[place], arrays[layer].at[place], item_pass.at[layer, 0], item_recv.at[layer, 0],
+                 {"section": 1 - layer})
+            for index, (source, target) in enumerate(smalls):
+                pltpu.make_async_copy(source, target.at[layer], small_sems.at[0, index]).start()
+                send(source, target.at[layer], small_sems.at[1, index], small_sems.at[2, index],
+                     {"section": 1 - layer})
+
+    units = [(layer, matrix) for layer in (0, 1) for matrix in range(4)]
+
+    def deep(unit):
+        layer, matrix = units[unit]
+
+        @pl.when(core == layer)
+        def unused():
+            for step in (1, 2, 3):
+                for half in (0, 1):
+                    for source, target in zip(
+                        raw_views(raw, matrix, half, place), whole_views(wholes[layer], matrix, place, depth)
+                    ):
+                        send(source, target, deep_send.at[unit], deep_recv.at[unit, step],
+                             {"section": half, "shard": lax.rem(depth + 4 - step, 4)})
+
+    def own(unit):
+        layer, matrix = units[unit]
+
+        @pl.when(core == layer)
+        def unused():
+            for quarter in range(4):
+                for source, target in zip(
+                    raw_views(raw, matrix, layer, quarter), whole_views(wholes[layer], matrix, quarter, depth)
+                ):
+                    pltpu.make_async_copy(source, target, own_send.at[unit, 0]).start()
+                for source, target in zip(
+                    raw_views(raw, matrix, 1 - layer, quarter), whole_views(wholes[layer], matrix, quarter, depth)
+                ):
+                    send(source, target, own_send.at[unit, 1], own_recv.at[unit], {"section": 1 - layer})
+
+    def route(unit, step):
+        return (1, 2) if (unit + step) % 2 == 0 else (2, 1)
+
+    def piece(unit, offset, step):
+        layer, matrix = units[unit]
+        return whole_view(wholes[layer], matrix, partner(place, offset), lax.rem(depth + step, 4))
+
+    def spread_first(unit):
+        for step in (1, 2, 3):
+            first, second = route(unit, step)
+            await_bytes(piece(unit, 0, step), deep_recv.at[unit, step])
+            for offset in (first, second):
+                send(piece(unit, 0, step), piece(unit, 0, step), hop_send.at[unit], hop_recv.at[unit, step - 1, offset - 1],
+                     {"dp": partner(place, offset)})
+
+    def spread_second(unit):
+        for step in (1, 2, 3):
+            first, second = route(unit, step)
+            await_bytes(piece(unit, first, step), hop_recv.at[unit, step - 1, first - 1])
+            send(piece(unit, first, step), piece(unit, first, step), hop_send.at[unit], hop_recv.at[unit, step - 1, 2],
+                 {"dp": partner(place, second)})
+
+    deep(0)
+    deep(1)
+    own(0)
+    own(1)
+    for unit in range(8):
+        if unit + 2 < 8:
+            deep(unit + 2)
+        spread_first(unit)
+        if unit + 2 < 8:
+            own(unit + 2)
+        if unit >= 1:
+            spread_second(unit - 1)
+        if unit in (0, 1):
+            layer = unit
+
+            @pl.when(core == layer)
+            def unused():
+                for step in (1, 2, 3):
+                    block = arrays[layer].at[partner(place, step)]
+                    await_bytes(block, item_recv.at[layer, step])
+                    send(block, block, item_pass.at[layer, step], item_recv.at[layer, step], {"section": 1 - layer})
+
+    spread_second(7)
+
+    for layer in (0, 1):
+        @pl.when(core == layer)
+        def unused():
+            for step in range(4):
+                await_bytes(items.at[0], item_send.at[layer, step])
+                await_bytes(items.at[0], item_pass.at[layer, step])
+            for index, (source, target) in enumerate(smalls):
+                await_bytes(source, small_sems.at[0, index])
+                await_bytes(source, small_sems.at[1, index])
+
+        @pl.when(core != layer)
+        def unused_too():
+            for step in range(4):
+                await_bytes(items.at[0], item_recv.at[layer, step])
+            for index, (source, target) in enumerate(smalls):
+                await_bytes(source, small_sems.at[2, index])
+
+    for unit, (layer, matrix) in enumerate(units):
+        whole = wholes[layer]
+        quarters = pieces_view(whole, matrix, 2, 2)
+
+        @pl.when(core == layer)
+        def unused():
+            await_bytes(quarters, own_send.at[unit, 0])
+            await_bytes(quarters, own_send.at[unit, 1])
+            await_bytes(pieces_view(whole, matrix, 3, 2), deep_send.at[unit])
+
+        @pl.when(core != layer)
+        def unused_too():
+            await_bytes(quarters, own_recv.at[unit])
+
+        for step in (1, 2, 3):
+            first, second = route(unit, step)
+            await_bytes(piece(unit, 0, 0), hop_recv.at[unit, step - 1, second - 1])
+            await_bytes(piece(unit, 0, 0), hop_recv.at[unit, step - 1, 2])
+        await_bytes(pieces_view(whole, matrix, 3, 3), hop_send.at[unit])
+
+
+def gather_all(*operands):
+    weights = (
+        array((4, 4, 256, 384), BF16),
+        array((4, 128, 1024), BF16),
+        array((4, 4, 256, 512), BF16),
+        array((4, 512, 1024), BF16),
+    )
+    shapes = (array((4, 256, 1024), BF16),) * 2 + weights * 2
+    shapes += tuple(array((2,) + operand.shape, F32) for operand in operands[5:])
+    anywhere = pl.BlockSpec(memory_space=pl.ANY)
+    dma = pltpu.SemaphoreType.DMA
+    return pl.pallas_call(
+        gather_kernel,
+        in_specs=[anywhere] * len(operands),
+        out_specs=[anywhere] * len(shapes),
+        out_shape=shapes,
+        scratch_shapes=[
+            dma((2, 4)), dma((2, 4)), dma((2, 4)), dma((8, 2)), dma((8,)),
+            dma((8,)), dma((8, 4)), dma((8,)), dma((8, 3, 3)), dma((3, 5)),
+        ],
+        compiler_params=pltpu.CompilerParams(collective_id=0, has_side_effects=True),
+    )(*operands)
+
+
+ORDER = tuple((layer, matrix) for layer in (1, 0) for matrix in (3, 2, 1, 0))
+
+
+def add_up_into(target, *terms):
+    rows = target.shape[0]
+
+    def step(index, unused):
+        span = pl.ds(pl.multiple_of(index * 32, 32), 32)
+        total = target[span, :].astype(F32)
+        for term in terms:
+            total = total + term[span, :].astype(F32)
+        target[span, :] = total.astype(BF16)
+        return unused
+
+    lax.fori_loop(0, rows // 32, step, 0)
+
+
+def reduce_kernel(*refs):
+    grads = (refs[0:4], refs[4:8])
+    smalls = (refs[8:13], refs[13:18])
+    ends_in = (refs[18], refs[19])
+    shares = refs[20:24]
+    ends, small_out = refs[24:26]
+    own, first_in, second_in, deep_in = refs[26:30], refs[30:34], refs[34:38], refs[38:42]
+    vec, inbox, acc = refs[42:45]
+    (load_sem, first_send, first_recv, second_send, second_recv, deep_send, deep_recv, last_send, last_copy,
+     last_recv, ends_send, ends_recv, small_send, small_recv) = refs[45:]
+    core, place, depth = here()
+    greet(core, place, depth)
+
+    for layer in (0, 1):
+        @pl.when(core == layer)
+        def unused():
+            source = ends_in[layer]
+            for step in (1, 2, 3):
+                send(source.at[partner(place, step)], ends.at[place], ends_send.at[step], ends_recv.at[step],
+                     {"dp": partner(place, step)})
+            pltpu.make_async_copy(source.at[place], ends.at[place], ends_send.at[0]).start()
+
+    def route(step):
+        return (1, 2) if step < 2 else (2, 1)
+
+    def shard_of(step):
+        return lax.rem(depth + step, 4)
+
+    def begin(unit):
+        layer, matrix = ORDER[unit]
+        for step in range(4):
+            first, second = route(step)
+            for index, offset in enumerate((first, 3)):
+                send(whole_view(grads[layer], matrix, partner(place, offset), shard_of(step)),
+                     first_in[matrix].at[layer, step, index], first_send.at[unit], first_recv.at[unit],
+                     {"dp": partner(place, first)})
+            for index, offset in enumerate((0, second)):
+                pltpu.make_async_copy(
+                    whole_view(grads[layer], matrix, partner(place, offset), shard_of(step)),
+                    own[matrix].at[layer, step, index], load_sem.at[unit],
+                ).start()
+
+    def second_hop(unit):
+        layer, matrix = ORDER[unit]
+        await_bytes(own[matrix].at[layer], load_sem.at[unit])
+        await_bytes(first_in[matrix].at[layer], first_recv.at[unit])
+        for step in range(4):
+            first, second = route(step)
+            mine = own[matrix].at[layer, step, 1]
+            add_up_into(mine, first_in[matrix].at[layer, step, 1])
+            send(mine, second_in[matrix].at[layer, step], second_send.at[unit], second_recv.at[unit],
+                 {"dp": partner(place, second)})
+
+    def deep_hop(unit):
+        layer, matrix = ORDER[unit]
+        await_bytes(second_in[matrix].at[layer], second_recv.at[unit])
+        for step in (1, 2, 3, 0):
+            mine = own[matrix].at[layer, step, 0]
+            add_up_into(mine, first_in[matrix].at[layer, step, 0], second_in[matrix].at[layer, step])
+            if step:
+                send(mine, deep_in[matrix].at[layer, step - 1], deep_send.at[unit], deep_recv.at[unit],
+                     {"shard": shard_of(step)})
+
+    def finish(unit):
+        layer, matrix = ORDER[unit]
+        await_bytes(deep_in[matrix].at[layer], deep_recv.at[unit])
+        mine = own[matrix].at[layer, 0, 0]
+        add_up_into(mine, *[deep_in[matrix].at[layer, index] for index in range(3)])
+        sources = [mine]
+        if matrix == 0:
+            sources = [mine.at[:, pl.ds(third * 128, 128)] for third in range(3)]
+        for half in (0, 1):
+            @pl.when(core == half)
+            def unused():
+                for source, target in zip(sources, raw_views(shares, matrix, half, place)):
+                    if half == layer:
+                        pltpu.make_async_copy(source, target, last_copy.at[unit]).start()
+                        for offset in (1, 2):
+                            send(source, target, last_send.at[unit, 0], last_recv.at[unit, half, offset],
+                                 {"dp": partner(place, offset)})
+                    else:
+                        send(source, target, last_send.at[unit, 0], last_recv.at[unit, half, 0], {"section": layer})
+
+    def forward(unit):
+        layer, matrix = ORDER[unit]
+        half = 1 - layer
+
+        @pl.when(core == layer)
+        def unused():
+            views = raw_views(shares, matrix, half, place)
+            await_bytes(own[matrix].at[layer, 0, 0], last_recv.at[unit, half, 0])
+            for view in views:
+                for offset in (1, 2):
+                    send(view, view, last_send.at[unit, 1], last_recv.at[unit, half, offset],
+                         {"dp": partner(place, offset)})
+
+    def corner(unit):
+        layer, matrix = ORDER[unit]
+
+        @pl.when(core == layer)
+        def unused():
+            for half in (layer, 1 - layer):
+                first, second = (1, 2) if half == 0 else (2, 1)
+                await_bytes(own[matrix].at[layer, 0, 0], last_recv.at[unit, half, first])
+                for view in raw_views(shares, matrix, half, partner(place, first)):
+                    send(view, view, last_send.at[unit, 2], last_recv.at[unit, half, 3], {"dp": partner(place, second)})
+
+    def clean(unit):
+        layer, matrix = ORDER[unit]
+        sample = own[matrix].at[layer, 0, 0]
+        await_bytes(first_in[matrix].at[layer], first_send.at[unit])
+        await_bytes(second_in[matrix].at[layer], second_send.at[unit])
+        await_bytes(deep_in[matrix].at[layer], deep_send.at[unit])
+
+        @pl.when(core == layer)
+        def unused():
+            await_bytes(sample, last_copy.at[unit])
+            for row in range(3):
+                await_bytes(own[matrix].at[layer, 0], last_send.at[unit, row])
+            for half in (0, 1):
+                first, second = (1, 2) if half == 0 else (2, 1)
+                await_bytes(sample, last_recv.at[unit, half, second])
+                await_bytes(sample, last_recv.at[unit, half, 3])
+
+        @pl.when(core != layer)
+        def unused_too():
+            await_bytes(sample, last_send.at[unit, 0])
+
+    vec[...] = jnp.zeros_like(vec)
+    column = pl.ds(pl.multiple_of(core * 512, 512), 512)
+    for layer in (0, 1):
+        entry_sums, norm_sums, mid_gain, mid_shift, heads = smalls[layer]
+
+        @pl.when(core == layer)
+        def unused():
+            vec[layer, 0:1, :] = entry_sums[0:1, :]
+            vec[layer, 1:3, :] = norm_sums[0:2, :]
+            vec[layer, 3:4, :] = entry_sums[1:2, :]
+            vec[layer, 4:6, :] = norm_sums[2:4, :]
+
+        vec[layer, 6:10, column] = mid_gain[...]
+        vec[layer, 10:14, column] = mid_shift[...]
+        vec[layer, 14:15, column] = heads[0:1, :]
+
+    exchanges = (
+        {"section": 1 - core},
+        {"dp": partner(place, 1)},
+        {"dp": partner(place, 2)},
+        {"shard": partner(depth, 1)},
+        {"shard": partner(depth, 2)},
+    )
+
+    def small_step(index):
+        if index:
+            source = acc.at[index - 1]
+            send(source, inbox.at[index], small_send.at[index], small_recv.at[index], exchanges[index])
+        else:
+            for half in (0, 1):
+                @pl.when(core == half)
+                def unused():
+                    send(vec.at[1 - half], inbox.at[0], small_send.at[0], small_recv.at[0], exchanges[0])
+
+    def small_take(index):
+        await_bytes(inbox.at[index], small_recv.at[index])
+        if index:
+            acc[index] = acc[index - 1] + inbox[index]
+        else:
+            for half in (0, 1):
+                @pl.when(core == half)
+                def unused():
+                    acc[0] = vec[half] + inbox[0]
+
+    begin(0)
+    begin(1)
+    small_step(0)
+    for turn in range(12):
+        if turn + 2 < 8:
+            begin(turn + 2)
+        if turn < 8:
+            second_hop(turn)
+        if 0 <= turn - 1 < 8:
+            deep_hop(turn - 1)
+        if 0 <= turn - 2 < 8:
+            finish(turn - 2)
+        if 0 <= turn - 3 < 8:
+            forward(turn - 3)
+        if 0 <= turn - 4 < 8:
+            corner(turn - 4)
+        if turn < 5:
+            small_take(turn)
+            if turn < 4:
+                small_step(turn + 1)
+    small_out[...] = acc[4]
+    for unit in range(8):
+        clean(unit)
+    for index in range(5):
+        await_bytes(inbox.at[index], small_send.at[index])
+    for step in range(4):
+        await_bytes(ends.at[0], ends_send.at[step])
+    for step in (1, 2, 3):
+        await_bytes(ends.at[0], ends_recv.at[step])
+
+
+def reduce_all(grads, smalls, ends):
+    anywhere = pl.BlockSpec(memory_space=pl.ANY)
+    local = pl.BlockSpec(memory_space=pltpu.VMEM)
+    dma = pltpu.SemaphoreType.DMA
+    operands = (*grads[0], *grads[1], *smalls[0], *smalls[1], *ends)
+    return pl.pallas_call(
+        reduce_kernel,
+        in_specs=[anywhere] * 8 + [local] * 10 + [anywhere] * 2,
+        out_specs=[anywhere] * 5 + [local],
+        out_shape=(
+            array((256, 3072), BF16),
+            array((256, 1024), BF16),
+            array((256, 4096), BF16),
+            array((1024, 1024), BF16),
+            array((4, 256, 1024), BF16),
+            array((16, 1024), F32),
+        ),
+        scratch_shapes=[pltpu.VMEM((2, 4, 2) + size, BF16) for size in SIZES]
+        + [pltpu.VMEM((2, 4, 2) + size, BF16) for size in SIZES]
+        + [pltpu.VMEM((2, 4) + size, BF16) for size in SIZES]
+        + [pltpu.VMEM((2, 3) + size, BF16) for size in SIZES]
+        + [pltpu.VMEM((2, 16, 1024), F32), pltpu.VMEM((5, 16, 1024), F32), pltpu.VMEM((5, 16, 1024), F32)]
+        + [dma((8,))] * 7
+        + [dma((8, 3)), dma((8,)), dma((8, 2, 4)), dma((4,)), dma((4,)), dma((5,)), dma((5,))],
+        compiler_params=pltpu.CompilerParams(
+            collective_id=1, has_side_effects=True, vmem_limit_bytes=VMEM_BYTES
+        ),
+    )(*operands)
+
+
+def local(
+    boundary,
+    first_len,
+    qkv_weight,
+    out_weight,
+    up_weight,
+    down_weight,
+    norm_gain,
+    norm_shift,
+    mid_gain,
+    mid_shift,
+    head_scale,
+):
+    core = lax.axis_index("section")
+    split_at = pick(first_len, lax.axis_index("dp"))
+    (x, cotangent, wq0, wo0, wu0, wd0, wq1, wo1, wu1, wd1, gains, shifts, mid_gains, mid_shifts, heads) = gather_all(
+        boundary[0, :, 0], qkv_weight[0], out_weight[0], up_weight[0], down_weight[0],
+        norm_gain[0], norm_shift[0], mid_gain, mid_shift, head_scale,
+    )
+    x, cotangent = x.reshape(1024, 1024), cotangent.reshape(1024, 1024)
+    weights = [
+        (wq.reshape(4, 1024, 384), wo.reshape(512, 1024), wu.reshape(4, 1024, 512), wd)
+        for wq, wo, wu, wd in ((wq0, wo0, wu0, wd0), (wq1, wo1, wu1, wd1))
+    ]
+
+    def own_half(value):
+        return lax.dynamic_index_in_dim(value, core, 2, keepdims=False)
+
+    mid_gains = own_half(mid_gains.reshape(2, 4, 2, 512))
+    mid_shifts = own_half(mid_shifts.reshape(2, 4, 2, 512))
+    heads = own_half(heads.reshape(2, 4, 2, 2))
+    smalls = [
+        (gains[layer], shifts[layer], mid_gains[layer], mid_shifts[layer], heads[layer]) for layer in (0, 1)
+    ]
+    projected = project(x, gains[0, 0:1], shifts[0, 0:1], weights[0][0])
+    residual, part, part_other, kept_first = layer_forward(projected, x, weights[0], smalls[0], split_at)
+    between, normed, proj = project_next(
+        residual, part, part_other, gains[1, 0:1], shifts[1, 0:1], weights[1][0]
+    )
+    residual, part, part_other, kept_second = layer_forward(
+        (normed, proj), between, weights[1], smalls[1], split_at
+    )
+    output = (residual + (part.astype(F32) + part_other.astype(F32))).astype(BF16)
+    d_between, big_second, small_second = layer_backward(cotangent, weights[1], smalls[1], kept_second)
+    d_x, big_first, small_first = layer_backward(d_between, weights[0], smalls[0], kept_first)
+    *shares, ends, totals = reduce_all(
+        (big_first, big_second),
+        (small_first, small_second),
+        (d_x.reshape(4, 256, 1024), output.reshape(4, 256, 1024)),
+    )
+    head_sums = jnp.sum(totals[14].reshape(2, 4, 2, 64), axis=3).transpose(1, 0, 2).reshape(1, 16)
+    return (
+        ends[None, :, None],
+        *[share.astype(F32)[None] for share in shares],
+        totals[0:3][None],
+        totals[3:6][None],
+        totals[6:10].reshape(1, 4096),
+        totals[10:14].reshape(1, 4096),
+        head_sums,
+    )
+
+
+def fits(mesh, boundary, mid_gain, head_scale):
+    sizes = (mesh.shape["section"], mesh.shape["dp"], mesh.shape["shard"])
+    return (
+        sizes == (2, 4, 4)
+        and boundary == (2, 4, 4, 1024, 1024)
+        and mid_gain == (2, 4096)
+        and head_scale == (2, 16)
+    )
+
+
 def solution(mesh):
     placed = (
         P("section", None, "shard", "dp", None),
@@ -286,21 +1331,24 @@
         P("section", None),
         P("section", None),
     )
-    return jax.shard_map(
-        local,
-        mesh=mesh,
-        in_specs=placed,
-        out_specs=(
-            P("section", None, "shard", "dp", None),
-            P("section", "shard", None),
-            P("section", "shard", None),
-            P("section", "shard", None),
-            P("section", "shard", None),
-            P("section", None, None),
-            P("section", None, None),
-            P("section", None),
-            P("section", None),
-            P("section", None),
-        ),
-        check_vma=False,
-    )
+    results = (
+        P("section", None, "shard", "dp", None),
+        P("section", "shard", None),
+        P("section", "shard", None),
+        P("section", "shard", None),
+        P("section", "shard", None),
+        P("section", None, None),
+        P("section", None, None),
+        P("section", None),
+        P("section", None),
+        P("section", None),
+    )
+
+    def whole(*arrays):
+        fast = fits(mesh, arrays[0].shape, arrays[8].shape, arrays[10].shape)
+        body = local if fast else general
+        return jax.shard_map(
+            body, mesh=mesh, in_specs=placed, out_specs=results, check_vma=False
+        )(*arrays)
+
+    return whole

time: 3580 us -> 899 us (0.25)
  waiting for transfers between devices: 2240 us -> 16.5 us
  Pallas kernels: 0 us -> 749 us
  matrix products: 786 us -> 54.5 us
  other arithmetic: 278 us -> 17.8 us
  local copies, waits for them, and re-layouts: 151 us -> 47.5 us
  blocking collectives: 76.8 us -> 0 us
    all_gather x24 -> x0, waiting for transfers between devices: 1030 us -> none  [the longest x10 303 us: forward_parts(): lax.all_gather(key_rows, 'dp', axis=0, tiled=True)]
    reduce_scatter x14 -> x0, waiting for transfers between devices: 1020 us -> none  [the longest x1 283 us: local(): lax.psum_scatter(big_sums[3][None], 'shard', scatter_dimension=1, tiled=T...]
    pallas_call x0 -> x22, Pallas kernels: none -> 749 us  [the longest x1 297 us: reduce_all(): pl.pallas_call(reduce_kernel, in_specs=[anywhere] * 8 + [local] * 10 + [a...]
    dot_general x115 -> x10, matrix products: 786 us -> 54.5 us  [the longest x2 16.9 us: layer_backward(): jnp.einsum('pmk,mn->pkn', middle, grad_low, preferred_element_type=F32)]
    psum x1 -> x0, waiting for transfers between devices: 173 us -> none  [local(): shares = lax.psum((shares[0], shares[1], shares[2], shares[3]), 'dp')]
    reduce_sum x95 -> x1, other arithmetic: 112 us -> 0.09 us  [local(): jnp.sum(totals[14].reshape(2, 4, 2, 64), axis=3).transpose(1, 0, 2)]
    convert_element_type x20 -> x1, other arithmetic: 97.8 us -> 5.47 us  [local(): (residual + (part.astype(F32) + part_other.astype(F32))).astype(BF16)]
    psum x1 -> x0, blocking collectives: 76.8 us -> none  [local(): lax.psum((small_sums[0], small_sums[1], small_sums[2], small_sums[3], sma...]
  transfers between devices with their start and end apart: 49 -> 12, of which waited for: 39 -> 7; matrix products, arithmetic and copies ran while one was open for 15% -> 9% of each run, Pallas kernels for 0% -> 3%
where the time goes in v1:
time: 899 us; the launch traced here: 895 us
  Pallas kernels  749 us (83%)
  matrix products  54.5 us (6%)
  local copies, waits for them, and re-layouts  47.5 us (5%)
  other arithmetic  17.8 us (2%)
  waiting for transfers between devices  16.5 us (2%)
    pallas_call x1, Pallas kernels, reduce_all(): pl.pallas_call(reduce_kernel, in_specs=[anywhere] * 8 + [local] * 10 + [a...  297 us
    pallas_call x1, Pallas kernels, gather_all(): pl.pallas_call(gather_kernel, in_specs=[anywhere] * len(operands), out_sp...  197 us
    pallas_call x2, Pallas kernels, attention_back(): pl.pallas_call(attend_back_kernel, grid_spec=pltpu.PrefetchScalarGridSpec...  41 us
    pallas_call x2, Pallas kernels, attention(): pl.pallas_call(attend_kernel, grid_spec=pltpu.PrefetchScalarGridSpec(num_...  40.4 us
    pallas_call x2, Pallas kernels, widen(): call_rows(kernel, (array((1024, 1024), F32), array((1024, 1024), BF16), w...  30.1 us
    pallas_call x2, Pallas kernels, norms_back(): call_rows(kernel, (array((1024, 1024), F32), array((1024, 1024), BF16), a...  25.7 us
    pallas_call x2, Pallas kernels, widen_back(): call_rows(kernel, (array((4, 1024, 512), BF16), array((1024, 1024), BF16)...  24.6 us
    pallas_call x2, Pallas kernels, narrow_back(): call_rows(kernel, (array((4, 1024, 512), BF16), array((1024, 128), F32),...  22.3 us
  transfers between devices with their start and end apart: 12, of which 7 were waited for; matrix products, arithmetic and copies ran while one was open for 9% of the time, Pallas kernels for 3%

profile of v1, /device:TPU:8, one launch (start us, length us, event | category | flops | bytes accessed | tf_op | source)
XLA Modules:
  0.0 894.6 jit_solution(9283220518074688626)
XLA Ops:
  0.7 1.3 copy.102
  2.0 1.3 copy.101
  3.3 196.5 %shard_map.186 = (bf16[4,256,1024]{2,1,0:T(8,128)(2,1)}, bf16[4,256,1024]{2,1,0:T(8,128)(2,1)}, bf16[4,4,256,384]{3,2,1,0:T(8,128)(2,1)}, bf16[4,128,1024]{2,1,0...) custom-call(bf16[4,256,1024]{2,1,0:T(8,128)(2,1)} %bitcast.145, ...), custom_call_target="tpu_custom_call" | custom-call | tf_op jit(solution)/shard_map/pallas_call | solution.py:985
  200.3 1.3 reduce.15
  203.8 1.4 slice_bitcast_fusion.8
  205.1 9.5 %shard_map.187 = (bf16[1024,1024]{1,0:T(8,128)(2,1)}, bf16[4,1024,384]{2,1,0:T(8,128)(2,1)}) custom-call(bf16[1024,1024]{1,0:T(8,128)(2,1)} %bitcast.138, f32[1,1024]{1,0:T(1,128)} %get-tuple-element.208.gain_ref, f32[1,1024]{1,0:T(1,128)} %get-tuple-element.201.shift_ref, bf16[4,1024,384]{2,1,0:T(8,128)(2,1)} %bitcast.169), custom_call_target="tpu_custom_call" | custom-call | flops 3221225472 | bytes 10485760 | tf_op jit(solution)/shard_map/pallas_call | solution.py:361
  214.6 20.2 %shard_map.188 = (bf16[1024,512]{1,0:T(8,128)(2,1)}, bf16[1024,512]{1,0:T(8,128)(2,1)}, f32[4,2,1024]{2,1,0:T(2,128)}) custom-call(s32[1]{0:T(128)} %bitcast.split_ref, bf16[4,1024,384]{2,1,0:T(8,128)(2,1)} %get-tuple-element.86.q_ref.k_ref.v_ref, bf16[4,1024,384]{2,1,0:T(8,128)(2,1)} %get-tuple-element.86.q_ref.k_ref.v_ref, ...), custom_call_target="tpu_custom_call" | custom-call | flops 20000000000 | bytes 8388608 | tf_op jit(solution)/shard_map/pallas_call | solution.py:435
  234.8 2.5 convolution_convert_fusion.3.a_ref.ba_ref
  237.4 3.8 collective-permute-start
  241.8 3.2 collective-permute-done.b_ref.bb_ref
  244.9 1.4 copy-done.3
  246.3 15.1 %shard_map.189 = (f32[1024,1024]{1,0:T(8,128)}, bf16[1024,1024]{1,0:T(8,128)(2,1)}, bf16[4,1024,512]{2,1,0:T(8,128)(2,1)}, bf16[4,1024,512]{2,1,0:T(8,128)(2,1)}, f32[1024,128]{1,0:T(8,128)}) custom-call(bf16[1024,1024]{1,0:T(8,128)(2,1)} %bitcast.139, bf16[1024,1024]{1,0:T(8,128)(2,1)} %copy-done.2, bf16[1024,1024]{1,0:T(8,128)(2,1)} %copy-done.3, ...), custom_call_target="tpu_custom_call" | custom-call | flops 4294967296 | bytes 31457280 | tf_op jit(solution)/shard_map/pallas_call | solution.py:547
  263.5 0.8 copy-done.16
  264.3 10.2 %shard_map.190 = (bf16[4,1024,512]{2,1,0:T(8,128)(2,1)}, bf16[1024,1024]{1,0:T(8,128)(2,1)}) custom-call(bf16[4,1024,512]{2,1,0:T(8,128)(2,1)} %get-tuple-element.93.g_ref, f32[1024,128]{1,0:T(8,128)} %get-tuple-element.94.own_ref, f32[1024,128]{1,0:T(8,128)} %copy-done.16, f32[4,512]{1,0:T(4,128)} %bitcast.156, f32[4,512]{1,0:T(4,128)} %bitcast.167, ...), custom_call_target="tpu_custom_call" | custom-call | flops 4294967296 | bytes 15728640 | tf_op jit(solution)/shard_map/pallas_call | solution.py:575
  275.6 3.3 collective-permute-done.2.b_ref
  278.9 1.4 copy-done.26
  280.2 11.2 %shard_map.191 = (bf16[1024,1024]{1,0:T(8,128)(2,1)}, bf16[1024,1024]{1,0:T(8,128)(2,1)}, bf16[4,1024,384]{2,1,0:T(8,128)(2,1)}) custom-call(f32[1024,1024]{1,0:T(8,128)} %get-tuple-element.92.res_ref, bf16[1024,1024]{1,0:T(8,128)(2,1)} %get-tuple-element.98.a_ref, bf16[1024,1024]{1,0:T(8,128)(2,1)} %copy-done.26, f32[1,1024]{1,0:T(1,128)} %get-tuple-element.209.gain_ref, ...), custom_call_target="tpu_custom_call" | custom-call | flops 3221225472 | bytes 18874368 | tf_op jit(solution)/shard_map/pallas_call | solution.py:381
  291.4 20.2 %shard_map.192 = (bf16[1024,512]{1,0:T(8,128)(2,1)}, bf16[1024,512]{1,0:T(8,128)(2,1)}, f32[4,2,1024]{2,1,0:T(2,128)}) custom-call(s32[1]{0:T(128)} %bitcast.split_ref, bf16[4,1024,384]{2,1,0:T(8,128)(2,1)} %get-tuple-element.101.q_ref.k_ref.v_ref, bf16[4,1024,384]{2,1,0:T(8,128)(2,1)} %get-tuple-element.101.q_ref.k_ref.v_ref, ...), custom_call_target="tpu_custom_call" | custom-call | flops 20000000000 | bytes 8388608 | tf_op jit(solution)/shard_map/pallas_call | solution.py:435
  311.6 2.5 convolution_convert_fusion.2.a_ref.ba_ref
  314.6 3.8 collective-permute-done.3.b_ref.bb_ref
  318.4 1.3 copy-done.7
  319.7 15.1 %shard_map.193 = (f32[1024,1024]{1,0:T(8,128)}, bf16[1024,1024]{1,0:T(8,128)(2,1)}, bf16[4,1024,512]{2,1,0:T(8,128)(2,1)}, bf16[4,1024,512]{2,1,0:T(8,128)(2,1)}, f32[1024,128]{1,0:T(8,128)}) custom-call(bf16[1024,1024]{1,0:T(8,128)(2,1)} %get-tuple-element.100.x_ref, bf16[1024,1024]{1,0:T(8,128)(2,1)} %copy-done.6, bf16[1024,1024]{1,0:T(8,128)(2,1)} %copy-done.7, ...), custom_call_target="tpu_custom_call" | custom-call | flops 4294967296 | bytes 31457280 | tf_op jit(solution)/shard_map/pallas_call | solution.py:547
  335.7 1.2 collective-permute-done.4.other_ref
  336.9 0.8 copy-done.17
  337.7 11.1 %shard_map.194 = (bf16[4,1024,512]{2,1,0:T(8,128)(2,1)}, f32[1024,128]{1,0:T(8,128)}, f32[4,512]{1,0:T(4,128)}, f32[4,512]{1,0:T(4,128)}) custom-call(bf16[1024,1024]{1,0:T(8,128)(2,1)} %bitcast.141, bf16[4,1024,512]{2,1,0:T(8,128)(2,1)} %get-tuple-element.106.g_ref, f32[1024,128]{1,0:T(8,128)} %get-tuple-element.107.own_ref, f32[1024,128]{1,0:T(8,128)} %copy-done.17, ...), custom_call_target="tpu_custom_call" | custom-call | flops 4294967296 | bytes 15728640 | tf_op jit(solution)/shard_map/pallas_call | solution.py:604
  349.2 1.8 collective-permute-done.5.b_ref
  351.0 0.8 copy-done.19
  351.8 12.4 %shard_map.195 = (bf16[4,1024,512]{2,1,0:T(8,128)(2,1)}, bf16[1024,1024]{1,0:T(8,128)(2,1)}) custom-call(bf16[4,1024,512]{2,1,0:T(8,128)(2,1)} %get-tuple-element.109.dm_ref, bf16[4,1024,512]{2,1,0:T(8,128)(2,1)} %get-tuple-element.106.g_ref, bf16[4,1024,512]{2,1,0:T(8,128)(2,1)} %get-tuple-element.110.s_ref, f32[1024,128]{1,0:T(8,128)} %get-tuple-element.107.own_ref, ...), custom_call_target="tpu_custom_call" | custom-call | flops 4294967296 | bytes 20971520 | tf_op jit(solution)/shard_map/pallas_call | solution.py:629
  365.4 3.2 collective-permute-done.6.db_ref
  368.5 1.3 copy-done.12
  369.9 12.9 %shard_map.196 = (f32[1024,1024]{1,0:T(8,128)}, bf16[1024,1024]{1,0:T(8,128)(2,1)}, bf16[1024,512]{1,0:T(8,128)(2,1)}, f32[8,1024]{1,0:T(8,128)}, f32[8,512]{1,0:T(8,128)}) custom-call(bf16[1024,1024]{1,0:T(8,128)(2,1)} %bitcast.142, f32[1024,1024]{1,0:T(8,128)} %get-tuple-element.105.res_ref, bf16[1024,1024]{1,0:T(8,128)(2,1)} %get-tuple-element.112.da_ref, ...), custom_call_target="tpu_custom_call" | custom-call | flops 1073741824 | bytes 26214400 | tf_op jit(solution)/shard_map/pallas_call | solution.py:658
  382.7 20.5 %shard_map.197.d_ref = bf16[4,1024,384]{2,1,0:T(8,128)(2,1)} custom-call(s32[1]{0:T(128)} %bitcast.split_ref, bf16[4,1024,384]{2,1,0:T(8,128)(2,1)} %get-tuple-element.101.q_ref.k_ref.v_ref, bf16[4,1024,384]{2,1,0:T(8,128)(2,1)} %get-tuple-element.101.q_ref.k_ref.v_ref, bf16[4,1024,384]{2,1,0:T(8,128)(2,1)} %get-tuple-element.101.q_ref.k_ref.v_ref, ...), custom_call_target="tpu_custom_call" | custom-call | flops 40000000000 | bytes 10485760 | tf_op jit(solution)/shard_map/pallas_call | solution.py:497
  403.2 8.2 shard_map.198.a_ref
  413.2 10.4 %shard_map.204 = (bf16[4,1024,512]{2,1,0:T(8,128)(2,1)}, bf16[1024,1024]{1,0:T(8,128)(2,1)}) custom-call(bf16[4,1024,512]{2,1,0:T(8,128)(2,1)} %get-tuple-element.106.g_ref, f32[1024,128]{1,0:T(8,128)} %get-tuple-element.107.own_ref, f32[1024,128]{1,0:T(8,128)} %copy-done.17, f32[4,512]{1,0:T(4,128)} %bitcast.161, f32[4,512]{1,0:T(4,128)} %bitcast.168, ...), custom_call_target="tpu_custom_call" | custom-call | flops 4294967296 | bytes 15728640 | tf_op jit(solution)/shard_map/pallas_call | solution.py:575
  423.7 8.5 convolution_convert_fusion.refs_7_
  432.3 1.4 copy-done.11
  433.6 7.3 shard_map.199
  440.9 11.2 %shard_map.200 = (bf16[4,1024,512]{2,1,0:T(8,128)(2,1)}, f32[1024,128]{1,0:T(8,128)}, f32[4,512]{1,0:T(4,128)}, f32[4,512]{1,0:T(4,128)}) custom-call(bf16[1024,1024]{1,0:T(8,128)(2,1)} %get-tuple-element.117.c_ref, bf16[4,1024,512]{2,1,0:T(8,128)(2,1)} %get-tuple-element.93.g_ref, f32[1024,128]{1,0:T(8,128)} %get-tuple-element.94.own_ref, ...), custom_call_target="tpu_custom_call" | custom-call | flops 4294967296 | bytes 15728640 | tf_op jit(solution)/shard_map/pallas_call | solution.py:604
  452.5 6.2 convert_bitcast_fusion
  458.7 6.4 copy.71
  465.1 5.5 add_convert_fusion
  470.6 0.8 copy-done.18
  471.4 12.1 %shard_map.201 = (bf16[4,1024,512]{2,1,0:T(8,128)(2,1)}, bf16[1024,1024]{1,0:T(8,128)(2,1)}) custom-call(bf16[4,1024,512]{2,1,0:T(8,128)(2,1)} %get-tuple-element.118.dm_ref, bf16[4,1024,512]{2,1,0:T(8,128)(2,1)} %get-tuple-element.93.g_ref, bf16[4,1024,512]{2,1,0:T(8,128)(2,1)} %get-tuple-element.119.s_ref, f32[1024,128]{1,0:T(8,128)} %get-tuple-element.94.own_ref, ...), custom_call_target="tpu_custom_call" | custom-call | flops 4294967296 | bytes 20971520 | tf_op jit(solution)/shard_map/pallas_call | solution.py:629
  483.7 5.6 convert_bitcast_fusion.2
  489.2 3.0 copy.69
  492.3 4.3 convolution_convert_fusion.4
  496.6 8.4 convolution_convert_fusion.1.refs_3_
  504.9 12.8 %shard_map.202 = (f32[1024,1024]{1,0:T(8,128)}, bf16[1024,1024]{1,0:T(8,128)(2,1)}, bf16[1024,512]{1,0:T(8,128)(2,1)}, f32[8,1024]{1,0:T(8,128)}, f32[8,512]{1,0:T(8,128)}) custom-call(bf16[1024,1024]{1,0:T(8,128)(2,1)} %get-tuple-element.117.c_ref, f32[1024,1024]{1,0:T(8,128)} %get-tuple-element.92.res_ref, bf16[1024,1024]{1,0:T(8,128)(2,1)} %get-tuple-element.121.da_ref, ...), custom_call_target="tpu_custom_call" | custom-call | flops 1073741824 | bytes 26214400 | tf_op jit(solution)/shard_map/pallas_call | solution.py:658
  517.7 20.5 %shard_map.203.d_ref = bf16[4,1024,384]{2,1,0:T(8,128)(2,1)} custom-call(s32[1]{0:T(128)} %bitcast.split_ref, bf16[4,1024,384]{2,1,0:T(8,128)(2,1)} %get-tuple-element.86.q_ref.k_ref.v_ref, bf16[4,1024,384]{2,1,0:T(8,128)(2,1)} %get-tuple-element.86.q_ref.k_ref.v_ref, bf16[4,1024,384]{2,1,0:T(8,128)(2,1)} %get-tuple-element.86.q_ref.k_ref.v_ref, ...), custom_call_target="tpu_custom_call" | custom-call | flops 40000000000 | bytes 10485760 | tf_op jit(solution)/shard_map/pallas_call | solution.py:497
  538.3 8.3 shard_map.205.a_ref
  547.0 6.4 convert_bitcast_fusion.1
  553.4 6.2 copy.66
  559.6 6.0 convert_bitcast_fusion.3
  565.6 2.8 copy.64
  568.4 4.2 convolution_convert_fusion.5
  572.5 7.2 shard_map.206
  579.8 296.5 %shard_map.207 = (bf16[256,3072]{1,0:T(8,128)(2,1)}, bf16[256,1024]{1,0:T(8,128)(2,1)}, bf16[256,4096]{1,0:T(8,128)(2,1)}, bf16[1024,1024]{1,0:T(8,128)(2,1)}, b...) custom-call(bf16[4,4,256,384]{3,2,1,0:T(8,128)(2,1)} %bitcast.129, bf16[4,128,1024]{2,1,0:T(8,128)(2,1)} %bitcast.132, ...), custom_call_target="tpu_custom_call" | custom-call | tf_op jit(solution)/shard_map/pallas_call | solution.py:1223
  877.1 0.8 slice_bitcast_fusion.2
  877.9 0.9 slice_bitcast_fusion
  882.1 2.3 bitcast_convert_fusion.3
  884.4 3.4 bitcast_convert_fusion.2
  887.8 2.5 bitcast_convert_fusion.1
  890.3 2.5 bitcast_convert_fusion
  892.8 1.3 copy.108
  (101 shorter events, 16.4 us)
Async XLA Ops:
  0.6 202.5 %copy-start = (s32[4,1]{0,1:T(1,128)S(1)}, s32[4,1]{0,1:T(1,128)}, u32[]{:S(2)}) copy-start(s32[4,1]{0,1:T(1,128)} %param.12) | copy-start | bytes 52
  214.6 20.2 %copy-start.14 = (bf16[4,128,1024]{2,1,0:T(8,128)(2,1)S(1)}, bf16[4,128,1024]{2,1,0:T(8,128)(2,1)}, u32[]{:S(2)}) copy-start(bf16[4,128,1024]{2,1,0:T(8,128)(2,1)} %get-tuple-element.90) | copy-start | bytes 3145732
  234.8 6.3 copy-start.20
  234.8 6.3 copy-start.21
  237.3 7.6 copy-start.2
  237.4 7.6 collective-permute-start
  244.9 1.4 copy-start.3
  246.3 15.4 %copy-start.23 = (f32[2,1,4096]{2,1,0:T(1,128)S(1)}, f32[2,1,4096]{2,1,0:T(1,128)}, u32[]{:S(2)}) copy-start(f32[2,1,4096]{2,1,0:T(1,128)} %get-tuple-element.95) | copy-start | bytes 98308
  246.3 15.5 %copy-start.22 = (f32[2,1,4096]{2,1,0:T(1,128)S(1)}, f32[2,1,4096]{2,1,0:T(1,128)}, u32[]{:S(2)}) copy-start(f32[2,1,4096]{2,1,0:T(1,128)} %get-tuple-element.96) | copy-start | bytes 98308
  261.4 2.1 collective-permute-start.1
  263.5 0.8 copy-start.16
  274.5 4.4 collective-permute-start.2
  278.9 1.4 copy-start.26
  291.4 20.2 %copy-start.15 = (bf16[4,128,1024]{2,1,0:T(8,128)(2,1)S(1)}, bf16[4,128,1024]{2,1,0:T(8,128)(2,1)}, u32[]{:S(2)}) copy-start(bf16[4,128,1024]{2,1,0:T(8,128)(2,1)} %get-tuple-element.103) | copy-start | bytes 3145732
  314.1 4.2 copy-start.6
  314.1 4.2 collective-permute-start.3
  318.4 1.3 copy-start.7
  334.8 2.1 collective-permute-start.4
  336.9 0.8 copy-start.17
  348.8 2.2 collective-permute-start.5
  351.0 0.8 copy-start.19
  364.2 4.4 collective-permute-start.6
  368.5 1.3 copy-start.12
  411.4 20.9 %collective-permute-start.7 = (bf16[1024,1024]{1,0:T(8,128)(2,1)}, bf16[1024,1024]{1,0:T(8,128)(2,1)S(1)}, u32[]{:S(2)}, u32[]{:S(2)}) collective-permute-start(bf16[1024,1024]{1,0:T(8,128)(2,1)} %shard_map.198.a_ref), channel_id=1, source_target_pairs={{0,16},{16,0},{1,17},{17,1},{2,18},{18,2},{3,19},{19,3},{4,20},{20... | collective-permute-start | bytes 6291464 | tf_op jit(solution)/shard_map/ppermute | solution.py:278
  413.2 10.5 %copy-start.4 = (bf16[4,256,1024]{2,1,0:T(8,128)(2,1)S(1)}, bf16[4,256,1024]{2,1,0:T(8,128)(2,1)}, u32[]{:S(2)}) copy-start(bf16[4,256,1024]{2,1,0:T(8,128)(2,1)} %get-tuple-element.87) | copy-start | bytes 6291460
  423.6 41.5 %collective-permute-start.11 = (bf16[1024,1024]{1,0:T(8,128)(2,1)}, bf16[1024,1024]{1,0:T(8,128)(2,1)}, u32[]{:S(2)}, u32[]{:S(2)}) collective-permute-start(bf16[1024,1024]{1,0:T(8,128)(2,1)} %get-tuple-element.147), channel_id=1, source_target_pairs={{0,16},{16,0},{1,17},{17,1},{2,18},{18,2},{3,19},{19,3},{4,20},{20... | collective-permute-start | bytes 6291464 | tf_op jit(solution)/shard_map/ppermute | solution.py:278
  432.3 1.4 copy-start.11
  440.9 11.7 %copy-start.24 = (bf16[4,1024,512]{2,1,0:T(8,128)(2,1)S(1)}, bf16[4,1024,512]{2,1,0:T(8,128)(2,1)}, u32[]{:S(2)}) copy-start(bf16[4,1024,512]{2,1,0:T(8,128)(2,1)} %get-tuple-element.132) | copy-start | bytes 12582916
  440.9 11.7 %copy-start.29 = (bf16[1024,1024]{1,0:T(8,128)(2,1)S(1)}, bf16[1024,1024]{1,0:T(8,128)(2,1)}, u32[]{:S(2)}) copy-start(bf16[1024,1024]{1,0:T(8,128)(2,1)} %get-tuple-element.133) | copy-start | bytes 6291460
  452.1 18.5 %collective-permute-start.8 = (f32[1024,128]{1,0:T(8,128)}, f32[1024,128]{1,0:T(8,128)S(1)}, u32[]{:S(2)}, u32[]{:S(2)}) collective-permute-start(f32[1024,128]{1,0:T(8,128)} %get-tuple-element.120.a_ref), channel_id=1, source_target_pairs={{0,16},{16,0},{1,17},{17,1},{2,18},{18,2},{3,19},{19,3},{4,20},{20... | collective-permute-start | bytes 1572872 | tf_op jit(solution)/shard_map/ppermute | solution.py:278
  458.7 6.4 copy-start.10
  470.6 0.8 copy-start.18
  471.4 12.3 %copy-start.27 = (bf16[1024,1024]{1,0:T(8,128)(2,1)S(1)}, bf16[1024,1024]{1,0:T(8,128)(2,1)}, u32[]{:S(2)}) copy-start(bf16[1024,1024]{1,0:T(8,128)(2,1)} %get-tuple-element.130) | copy-start | bytes 6291460
  483.5 21.4 %collective-permute-start.9 = (bf16[1024,1024]{1,0:T(8,128)(2,1)}, bf16[1024,1024]{1,0:T(8,128)(2,1)}, u32[]{:S(2)}, u32[]{:S(2)}) collective-permute-start(bf16[1024,1024]{1,0:T(8,128)(2,1)} %get-tuple-element.121.da_ref), channel_id=1, source_target_pairs={{0,16},{16,0},{1,17},{17,1},{2,18},{18,2},{3,19},{19,3},{4,20},{20... | collective-permute-start | bytes 6291464 | tf_op jit(solution)/shard_map/ppermute | solution.py:278
  492.3 4.3 copy-start.5
  538.3 8.7 copy-start.25
  538.3 8.7 copy-start.28
  546.6 25.9 %collective-permute-start.10 = (bf16[1024,1024]{1,0:T(8,128)(2,1)}, bf16[1024,1024]{1,0:T(8,128)(2,1)}, u32[]{:S(2)}, u32[]{:S(2)}) collective-permute-start(bf16[1024,1024]{1,0:T(8,128)(2,1)} %shard_map.205.a_ref), channel_id=1, source_target_pairs={{0,16},{16,0},{1,17},{17,1},{2,18},{18,2},{3,19},{19,3},{4,20},{20... | collective-permute-start | bytes 6291464 | tf_op jit(solution)/shard_map/ppermute | solution.py:278
  882.1 5.7 copy-start.9
  887.8 2.5 copy-start.8
  890.3 2.5 copy-start.13
  890.3 3.8 copy-start.1
